TPU v7x, 1024 devices: a whole 8x8x8 slice. The times are simulated.
1024 devices in a mesh: gx: 4 (over y_lo, core), gy: 4 (over y_hi), gz: 64 (over z, x).
Axes of the slice: x: 8, y: 8 (y_hi: 4, y_lo: 2; y = y_hi * 2 + y_lo), z: 8, core: 2. Of those that a mesh axis runs over, the one named last changes fastest.
Arguments:
- offsets: float32 [3, 4, 8, 128, 128], P(None, 'gx', 'gy', 'gz'), may hold values from 0 to 11, as said below
- type_ids: int32 [4, 8, 128, 128], P('gx', 'gy', 'gz'), may hold values from 0 to 1
- neighbours: int32 [4, 8, 128, 27], P('gx', 'gy', 'gz'), may hold values from 0 to 48, as said below
- type_chi: float32 [2], replicated, may hold values from 3 to 7
- type_eta: float32 [2], replicated, may hold values from 6 to 12
- type_gamma: float32 [2], replicated, may hold values from 0.5 to 1
Outputs:
- charges: float32 [4, 8, 128, 128], P('gx', 'gy', 'gz')
- residuals: float32 [2, 4, 8, 128, 128], P(None, 'gx', 'gy', 'gz')
Inputs may be any that keep to these rules, and one draw needn't show every extreme that they name: `neighbours`: each tile's row lists the tile itself and some of the 26 cells around it, each at most once, as indices into its device's block padded by one cell on every side (3) x (4) x (4) in first-dimension-major order; unused slots hold (3) * 4 * 4. Two tiles list each other with opposite displacements or not at all. `offsets`: any two atoms of the box lie at least 0.8 A apart.
All inputs are finite; a program needn't handle non-finite values.
Results may differ from a plain program's by a relative error of at most 0.0003.
Values sent between devices are 32-bit elements; how exact they have to be, the bound alone decides.
No kernel may reach another device: no remote copies, remote signals or barrier semaphores. Data moves between devices by JAX's collectives and lax.ppermute only.
A program may use at most 32 MiB of HBM per device.

v0:
```python
import jax
import jax.numpy as jnp
from jax import lax
from jax.sharding import Mesh
from jax.sharding import PartitionSpec as P

ITERS = 3
GX_GY_GZ = ("gx_0", "gx_1", "gy", "gz_0", "gz_1")
GX = ("gx_0", "gx_1")
GZ = ("gz_0", "gz_1")


CELL_EDGE = 11.0
CUTOFF = 10.0
COULOMB = 14.4


def extended(cells, sides, width):
    for axis, dim in sides:
        count = lax.axis_size(axis)
        head = lax.slice_in_dim(cells, 0, width, axis=dim)
        tail = lax.slice_in_dim(cells, cells.shape[dim] - width, cells.shape[dim], axis=dim)
        cells = jnp.concatenate(
            [
                lax.ppermute(tail, axis, [(i, (i + 1) % count) for i in range(count)]),
                cells,
                lax.ppermute(head, axis, [((i + 1) % count, i) for i in range(count)]),
            ],
            axis=dim,
        )
    return cells


def over_axes(shard, axes):
    for axis in axes:
        shard = lax.psum(shard, axis)
    return shard


def taper_value(distance):
    scaled = distance / CUTOFF
    squared = scaled * scaled
    return 1.0 + squared * squared * (-35.0 + scaled * (84.0 + scaled * (-70.0 + scaled * 20.0)))


def couplings(own_pos, own_shield, near_pos, near_shield, shifts, listed, itself):
    displace = near_pos[:, :, None, :] + shifts[:, :, None, None] - own_pos[:, None, :, None]
    dist_sq = jnp.sum(displace * displace, axis=0)
    distance = jnp.sqrt(dist_sq)
    screen = own_shield[None, :, None] * near_shield[:, None, :]
    kernel = COULOMB * taper_value(distance) / jnp.cbrt(dist_sq * distance + screen)
    diagonal_mask = jnp.eye(own_pos.shape[1], dtype=bool)
    retained = (
        listed[:, None, None]
        & (distance < CUTOFF)
        & jnp.logical_not(itself[:, None, None] & diagonal_mask[None])
    )
    return jnp.where(retained, kernel, jnp.zeros_like(kernel))


def table_lookup(type_ids, table):
    result = jnp.zeros(type_ids.shape, table.dtype)
    for kind_index in range(table.shape[0]):
        result = jnp.where(type_ids == kind_index, table[kind_index], result)
    return result


def decode_cells(entries, local_one, local_two, local_three, width_two, width_three):
    plane_cells = (width_two + 2) * (width_three + 2)
    step_one = entries // plane_cells - 1 - local_one[..., None]
    step_two = entries // (width_three + 2) % (width_two + 2) - 1 - local_two[..., None]
    step_three = entries % (width_three + 2) - 1 - local_three[..., None]
    return (step_one, step_two, step_three)


def summed_over(values):
    return jnp.sum(values, axis=(1, 2))


def per_device(offsets, type_ids, neighbours, type_chi, type_eta, type_gamma):
    cells_one, cells_two, cells_three, atoms_tile = offsets.shape[1:]
    tiles = cells_one * cells_two * cells_three
    slots = neighbours.shape[-1]
    sentinel = (cells_one + 2) * (cells_two + 2) * (cells_three + 2)
    chi_atom = table_lookup(type_ids, type_chi)
    eta_atom = table_lookup(type_ids, type_eta)
    shield = table_lookup(type_ids, type_gamma ** (-1.5))
    source = jnp.stack([-chi_atom, -jnp.ones_like(chi_atom)])
    fields = jnp.concatenate([offsets, shield[None], -chi_atom[None]], 0)
    padded = extended(fields, ((GX, 1), ("gy", 2), (GZ, 3)), 1)
    source_ghosts = jnp.stack([padded[4], -jnp.ones_like(padded[4])])

    def flatten(stacked):
        reshaped = stacked.reshape(stacked.shape[0], sentinel, atoms_tile)
        return jnp.concatenate(
            [reshaped, jnp.zeros((stacked.shape[0], 1, atoms_tile), stacked.dtype)], 1
        )

    pos_all = flatten(padded[0:3])
    shield_all = flatten(padded[3:4])[0]
    shape_grid = (cells_one, cells_two, cells_three)
    local_one = jnp.broadcast_to(jnp.arange(cells_one, dtype=jnp.int32)[:, None, None], shape_grid)
    local_two = jnp.broadcast_to(jnp.arange(cells_two, dtype=jnp.int32)[None, :, None], shape_grid)
    local_three = jnp.broadcast_to(
        jnp.arange(cells_three, dtype=jnp.int32)[None, None, :], shape_grid
    )
    step_one, step_two, step_three = decode_cells(
        neighbours, local_one, local_two, local_three, cells_two, cells_three
    )
    listed = (neighbours != sentinel).reshape(tiles, slots)
    itself = ((step_one == 0) & (step_two == 0) & (step_three == 0)).reshape(tiles, slots)
    shifts = (
        jnp.stack([step_one, step_two, step_three], axis=-2)
        .reshape(tiles, 3, slots)
        .astype(jnp.float32)
        * CELL_EDGE
    )
    row_index = neighbours.reshape(tiles, slots)
    own_pos = jnp.moveaxis(offsets.reshape(3, tiles, atoms_tile), 1, 0)
    own_shield = shield.reshape(tiles, atoms_tile)

    def build_tile(tile_item):
        own_block, own_screen, indices, shifted, valid_slot, selfish = tile_item
        return couplings(
            own_block,
            own_screen,
            pos_all[:, indices],
            shield_all[indices],
            shifted,
            valid_slot,
            selfish,
        )

    blocks = lax.map(build_tile, (own_pos, own_shield, row_index, shifts, listed, itself))
    diagonal = eta_atom.reshape(tiles, atoms_tile)

    def apply_padded(local_part, ghosts):
        values = flatten(ghosts)[:, row_index]
        return diagonal[None] * local_part + jnp.einsum(
            "tsij,ctsj->cti", blocks, values, precision=lax.Precision.HIGHEST
        )

    def products(residual, image_now, solution, direction):
        return (
            over_axes(summed_over(residual * residual), GX_GY_GZ),
            over_axes(summed_over(residual * image_now), GX_GY_GZ),
            over_axes(summed_over(solution), GX_GY_GZ),
            over_axes(summed_over(residual), GX_GY_GZ),
            over_axes(summed_over(direction), GX_GY_GZ),
        )

    residual = source.reshape(2, tiles, atoms_tile)
    solution = jnp.zeros_like(residual)
    image_now = apply_padded(residual, source_ghosts)
    norm_now, curvature, unused_one, unused_two, unused_three = products(
        residual, image_now, solution, residual
    )
    step_size = norm_now / curvature
    direction = residual
    along_image = image_now
    carried = (norm_now, norm_now, norm_now, norm_now, step_size)
    for iteration in range(ITERS):
        solution = solution + step_size[:, None, None] * direction
        residual = residual - step_size[:, None, None] * along_image
        if iteration + 1 < ITERS:
            shaped = residual.reshape(2, cells_one, cells_two, cells_three, atoms_tile)
            apply_ghosts = extended(shaped, ((GX, 1), ("gy", 2), (GZ, 3)), 1)
            image_now = apply_padded(residual, apply_ghosts)
            norm_next, curvature, sum_solution, sum_residual, sum_direction = products(
                residual, image_now, solution, direction
            )
            growth = norm_next / norm_now
            step_size = norm_next / (curvature - growth * norm_next / step_size)
            direction = residual + growth[:, None, None] * direction
            along_image = image_now + growth[:, None, None] * along_image
            norm_now = norm_next
            carried = (sum_solution, sum_residual, sum_direction, growth, step_size)
    sum_solution, sum_residual, sum_direction, growth, last_step = carried
    totals = sum_solution + last_step * (sum_residual + growth * sum_direction)
    charges = 1000.0 * (solution[0] - totals[0] / totals[1] * solution[1])
    return (
        charges.reshape(cells_one, cells_two, cells_three, atoms_tile),
        residual.reshape(2, cells_one, cells_two, cells_three, atoms_tile),
    )


def solution(mesh):
    torus = Mesh(
        mesh.devices.reshape(2, 2, mesh.shape["gy"], 8, 8), ("gx_0", "gx_1", "gy", "gz_0", "gz_1")
    )
    in_specs = (
        P(None, GX, "gy", GZ, None),
        P(GX, "gy", GZ, None),
        P(GX, "gy", GZ, None),
        P(),
        P(),
        P(),
    )
    out_specs = (P(GX, "gy", GZ, None), P(None, GX, "gy", GZ, None))
    return jax.shard_map(
        per_device, mesh=torus, in_specs=in_specs, out_specs=out_specs, check_vma=False
    )
```

profile of v0, /device:TPU:16, one launch (start us, length us, event | category | flops | bytes accessed | tf_op | source)
XLA Modules:
  0.0 332.0 jit_solution(15220835933969070373)
XLA Ops:
  16.8 10.6 %collective-permute-done.1 = f32[5,1,2,2,128]{4,3,2,1,0:T(2,128)S(1)} collective-permute-done((f32[5,1,2,2,128]{4,3,2,1,0:T(2,128)S(1)}, f32[5,1,2,2,128]{4,3,2,1,0:T(2,128)S(1)}, u32[]{:S(2)}, u32[]{:S(2)}) %collective-permute-start.1) | collective-permute-done | bytes 10272 | tf_op jit(solution)/shard_map/ppermute | solution.py:27
  30.0 6.0 %collective-permute-start.3 = (f32[5,3,1,2,128]{4,3,2,1,0:T(2,128)S(1)}, f32[5,3,1,2,128]{4,3,2,1,0:T(2,128)S(1)}, u32[]{:S(2)}, u32[]{:S(2)}) collective-permute-start(f32[5,3,1,2,128]{4,3,2,1,0:T(2,128)S(1)} %get-tuple-element.255), channel_id=1, source_target_pairs={{64,0},{128,64},{192,128},{0,192},{65,1},{129,65},{193,129},{1,193... | collective-permute-start | bytes 46088 | tf_op jit(solution)/shard_map/ppermute | solution.py:27
  40.2 11.1 %collective-permute-start.5 = (f32[5,3,4,1,128]{4,3,2,1,0:T(1,128)S(1)}, f32[5,3,4,1,128]{4,3,2,1,0:T(1,128)S(1)}, u32[]{:S(2)}, u32[]{:S(2)}) collective-permute-start(f32[5,3,4,1,128]{4,3,2,1,0:T(1,128)S(1)} %get-tuple-element.253), channel_id=1, source_target_pairs={{1,0},{2,1},{3,2},{4,3},{5,4},{6,5},{7,6},{8,7},{9,8},{10,9},{11,1... | collective-permute-start | bytes 92168 | tf_op jit(solution)/shard_map/ppermute | solution.py:27
  53.8 29.4 %while.12 = (s32[]{:T(128)}, f32[4,27,128,128]{3,2,1,0:T(8,128)}, pred[4,27]{1,0:T(4,128)(4,1)S(1)}, s32[4,27]{1,0:T(4,128)}, f32[3,49,128]{2,0,1:T(4,128)S(1)},...) while((s32[]{:T(128)}, f32[4,27,128,128]{3,2,1,0:T(8,128)}, ...), condition=%wide.region_8.9_spmd, body=%wide.region_6.8_spmd.sunk | while | flops 13298899 | bytes 5686811 | solution.py:134
  78.7 4.5 %fusion.66 = f32[4,27,128,128]{3,2,1,0:T(8,128)} fusion(f32[4,27,128,128]{3,2,1,0:T(8,128)} %get-tuple-element.360, s32[]{:T(128)} %get-tuple-element.359, f32[27,128,128]{2,1,0:T(8,128)S(1)} %multiply_reduce_fusion.7, f32[27,128]{1,0:T(8,128)S(1)} %gather_fusion.1, f32[128]{0:T(128)S(1)} %fusion.65, pred[27]{0:T(512)(128)(4,1)S(1)} %get-tuple-element.346, ...), kind=kLoop, calls=%fused_computation.21.clone.1 | loop fusion | flops 9732096 | bytes 3570230 | tf_op jit(solution)/shard_map/while/body/jit(dynamic_update_index_in_dim)/dynamic_update_slice | solution.py:134
  83.9 8.3 %fusion.24 = (f32[2]{0:T(128)S(1)}, f32[2,4,128]{2,0,1:T(2,128)S(1)}) fusion(f32[2,1,2,2,128]{4,0,3,2,1:T(2,128)S(1)} %stack.24.clone, f32[2,4,128]{2,0,1:T(2,128)S(1)} %bitcast_multiply_fusion.3, f32[2,4,27,128]{3,0,2,1:T(2,128)S(1)} %bitcast.130, f32[4,27,128,128]{3,2,1,0:T(8,128)} %get-tuple-element.127), kind=kOutput, calls=%fused_computation.69 | convolution fusion | flops 42470400 | bytes 7200776 | tf_op jit(solution)/shard_map/tsij,ctsj->cti/dot_general | solution.py:139
  92.3 4.9 %all-reduce.21 = (f32[2]{0:T(128)S(1)}, f32[2]{0:T(128)S(1)}) all-reduce(f32[2]{0:T(128)S(1)} %multiply_reduce_fusion.5, f32[2]{0:T(128)S(1)} %get-tuple-element.279), channel_id=1, replica_groups=mesh['gx_0'=2,'gx_1'=2,'gy'=4,'gz_0'=8,'gz_1'=8] {'gx_0'}, use_global_device_ids=true, to_apply=%region_1.2 | all-reduce | flops 4 | bytes 32 | tf_op jit(solution)/shard_map/psum | solution.py:36
  99.7 12.9 %all-reduce.15 = (f32[2]{0:T(128)S(1)}, f32[2]{0:T(128)S(1)}) all-reduce(f32[2]{0:T(128)S(1)} %get-tuple-element.223, f32[2]{0:T(128)S(1)} %get-tuple-element.224), channel_id=1, replica_groups=mesh['gx_0'=2,'gx_1'=2,'gy'=4,'gz_0'=8,'gz_1'=8] {'gy'}, use_global_device_ids=true, to_apply=%region_3.4 | all-reduce | flops 4 | bytes 32 | tf_op jit(solution)/shard_map/psum | solution.py:36
  112.5 15.9 %all-reduce.12 = (f32[2]{0:T(128)S(1)}, f32[2]{0:T(128)S(1)}) all-reduce(f32[2]{0:T(128)S(1)} %get-tuple-element.214, f32[2]{0:T(128)S(1)} %get-tuple-element.215), channel_id=1, replica_groups=mesh['gx_0'=2,'gx_1'=2,'gy'=4,'gz_0'=8,'gz_1'=8] {'gz_0'}, use_global_device_ids=true, to_apply=%region_4.5 | all-reduce | flops 4 | bytes 32 | tf_op jit(solution)/shard_map/psum | solution.py:36
  128.5 18.5 %all-reduce.9 = (f32[2]{0:T(128)S(1)}, f32[2]{0:T(128)S(1)}) all-reduce(f32[2]{0:T(128)S(1)} %get-tuple-element.205, f32[2]{0:T(128)S(1)} %get-tuple-element.206), channel_id=1, replica_groups=mesh['gx_0'=2,'gx_1'=2,'gy'=4,'gz_0'=8,'gz_1'=8] {'gz_1'}, use_global_device_ids=true, to_apply=%region_5.6 | all-reduce | flops 4 | bytes 32 | tf_op jit(solution)/shard_map/psum | solution.py:36
  155.9 6.0 %collective-permute-start.9 = (f32[2,3,1,2,128]{4,0,3,2,1:T(2,128)S(1)}, f32[2,3,1,2,128]{4,0,3,2,1:T(2,128)S(1)}, u32[]{:S(2)}, u32[]{:S(2)}) collective-permute-start(f32[2,3,1,2,128]{4,0,3,2,1:T(2,128)S(1)} %get-tuple-element.263), channel_id=1, source_target_pairs={{64,0},{128,64},{192,128},{0,192},{65,1},{129,65},{193,129},{1,193... | collective-permute-start | bytes 18440 | tf_op jit(solution)/shard_map/ppermute | solution.py:27
  165.5 7.4 %collective-permute-start.11 = (f32[2,3,4,1,128]{4,0,3,2,1:T(2,128)S(1)}, f32[2,3,4,1,128]{4,0,3,2,1:T(2,128)S(1)}, u32[]{:S(2)}, u32[]{:S(2)}) collective-permute-start(f32[2,3,4,1,128]{4,0,3,2,1:T(2,128)S(1)} %get-tuple-element.259), channel_id=1, source_target_pairs={{1,0},{2,1},{3,2},{4,3},{5,4},{6,5},{7,6},{8,7},{9,8},{10,9},{11,1... | collective-permute-start | bytes 36872 | tf_op jit(solution)/shard_map/ppermute | solution.py:27
  174.9 8.3 %multiply_reduce_fusion.3 = (f32[2]{0:T(128)S(1)}, f32[2]{0:T(128)S(1)}, f32[2,4,128]{2,0,1:T(2,128)S(1)}) fusion(f32[2,4,128]{2,0,1:T(2,128)S(1)} %bitcast_subtract_fusion, f32[2,4,27,128]{3,0,2,1:T(2,128)S(1)} %bitcast.132, f32[4,27,128,128]{3,2,1,0:T(8,128)} %get-tuple-element.127, f32[4,128]{1,0:T(4,128)S(1)} %bitcast.157), kind=kOutput, calls=%fused_computation.78 | convolution fusion | flops 42473468 | bytes 7198736 | tf_op jit(solution)/shard_map/tsij,ctsj->cti/dot_general | solution.py:139
  183.2 4.9 %all-reduce.20 = (f32[2]{0:T(128)S(1)}, f32[2]{0:T(128)S(1)}) all-reduce(f32[2]{0:T(128)S(1)} %get-tuple-element.168, f32[2]{0:T(128)S(1)} %get-tuple-element.167), channel_id=1, replica_groups=mesh['gx_0'=2,'gx_1'=2,'gy'=4,'gz_0'=8,'gz_1'=8] {'gx_0'}, use_global_device_ids=true, to_apply=%region_16.17 | all-reduce | flops 4 | bytes 32 | tf_op jit(solution)/shard_map/psum | solution.py:36
  190.6 12.7 %all-reduce.14 = (f32[2]{0:T(128)S(1)}, f32[2]{0:T(128)S(1)}) all-reduce(f32[2]{0:T(128)S(1)} %get-tuple-element.221, f32[2]{0:T(128)S(1)} %get-tuple-element.222), channel_id=1, replica_groups=mesh['gx_0'=2,'gx_1'=2,'gy'=4,'gz_0'=8,'gz_1'=8] {'gy'}, use_global_device_ids=true, to_apply=%region_18.19 | all-reduce | flops 4 | bytes 32 | tf_op jit(solution)/shard_map/psum | solution.py:36
  203.4 14.1 %all-reduce.11 = (f32[2]{0:T(128)S(1)}, f32[2]{0:T(128)S(1)}) all-reduce(f32[2]{0:T(128)S(1)} %get-tuple-element.212, f32[2]{0:T(128)S(1)} %get-tuple-element.213), channel_id=1, replica_groups=mesh['gx_0'=2,'gx_1'=2,'gy'=4,'gz_0'=8,'gz_1'=8] {'gz_0'}, use_global_device_ids=true, to_apply=%region_19.20 | all-reduce | flops 4 | bytes 32 | tf_op jit(solution)/shard_map/psum | solution.py:36
  217.5 20.3 %all-reduce.8 = (f32[2]{0:T(128)S(1)}, f32[2]{0:T(128)S(1)}) all-reduce(f32[2]{0:T(128)S(1)} %get-tuple-element.203, f32[2]{0:T(128)S(1)} %get-tuple-element.204), channel_id=1, replica_groups=mesh['gx_0'=2,'gx_1'=2,'gy'=4,'gz_0'=8,'gz_1'=8] {'gz_1'}, use_global_device_ids=true, to_apply=%region_20.21 | all-reduce | flops 4 | bytes 32 | tf_op jit(solution)/shard_map/psum | solution.py:36
  246.8 6.0 %collective-permute-start.15 = (f32[2,3,1,2,128]{4,0,3,2,1:T(2,128)S(1)}, f32[2,3,1,2,128]{4,0,3,2,1:T(2,128)S(1)}, u32[]{:S(2)}, u32[]{:S(2)}) collective-permute-start(f32[2,3,1,2,128]{4,0,3,2,1:T(2,128)S(1)} %get-tuple-element.261), channel_id=1, source_target_pairs={{64,0},{128,64},{192,128},{0,192},{65,1},{129,65},{193,129},{1,193... | collective-permute-start | bytes 18440 | tf_op jit(solution)/shard_map/ppermute | solution.py:27
  256.4 7.2 %collective-permute-start.17 = (f32[2,3,4,1,128]{4,0,3,2,1:T(2,128)S(1)}, f32[2,3,4,1,128]{4,0,3,2,1:T(2,128)S(1)}, u32[]{:S(2)}, u32[]{:S(2)}) collective-permute-start(f32[2,3,4,1,128]{4,0,3,2,1:T(2,128)S(1)} %get-tuple-element.257), channel_id=1, source_target_pairs={{1,0},{2,1},{3,2},{4,3},{5,4},{6,5},{7,6},{8,7},{9,8},{10,9},{11,1... | collective-permute-start | bytes 36872 | tf_op jit(solution)/shard_map/ppermute | solution.py:27
  265.8 8.3 %fusion.35 = (f32[2]{0:T(128)S(1)}, f32[2]{0:T(128)S(1)}, f32[2]{0:T(128)S(1)}, f32[2,4,128]{2,0,1:T(2,128)S(1)}) fusion(f32[2,4,128]{2,0,1:T(2,128)S(1)} %get-tuple-element.266, f32[2,4,27,128]{3,0,2,1:T(2,128)S(1)} %bitcast.131, f32[4,27,128,128]{3,2,1,0:T(8,128)} %get-tuple-element.127, f32[4,128]{1,0:T(4,128)S(1)} %bitcast.158), kind=kOutput, calls=%fused_computation.113 | convolution fusion | flops 42474488 | bytes 7198744 | tf_op jit(solution)/shard_map/tsij,ctsj->cti/dot_general | solution.py:139
  274.2 4.9 %all-reduce.19 = (f32[2]{0:T(128)S(1)}, f32[2]{0:T(128)S(1)}, f32[2]{0:T(128)S(1)}, f32[2]{0:T(128)S(1)}, f32[2]{0:T(128)S(1)}) all-reduce(f32[2]{0:T(128)S(1)} %get-tuple-element.166, f32[2]{0:T(128)S(1)} %get-tuple-element.165, f32[2]{0:T(128)S(1)} %get-tuple-element.239, ...), channel_id=1, replica_groups=mesh['gx_0'=2,'gx_1'=2,'gy'=4,'gz_0'=8,'gz_1'=8] {'gx_0'}, use_global_device_ids=true, to_apply=%region_28.29 | all-reduce | flops 10 | bytes 80 | tf_op jit(solution)/shard_map/psum | solution.py:36
  281.6 12.7 %all-reduce.13 = (f32[2]{0:T(128)S(1)}, f32[2]{0:T(128)S(1)}, f32[2]{0:T(128)S(1)}, f32[2]{0:T(128)S(1)}, f32[2]{0:T(128)S(1)}) all-reduce(f32[2]{0:T(128)S(1)} %get-tuple-element.216, f32[2]{0:T(128)S(1)} %get-tuple-element.217, f32[2]{0:T(128)S(1)} %get-tuple-element.218, ...), channel_id=1, replica_groups=mesh['gx_0'=2,'gx_1'=2,'gy'=4,'gz_0'=8,'gz_1'=8] {'gy'}, use_global_device_ids=true, to_apply=%region_30.31 | all-reduce | flops 10 | bytes 80 | tf_op jit(solution)/shard_map/psum | solution.py:36
  294.3 14.2 %all-reduce.10 = (f32[2]{0:T(128)S(1)}, f32[2]{0:T(128)S(1)}, f32[2]{0:T(128)S(1)}, f32[2]{0:T(128)S(1)}, f32[2]{0:T(128)S(1)}) all-reduce(f32[2]{0:T(128)S(1)} %get-tuple-element.207, f32[2]{0:T(128)S(1)} %get-tuple-element.208, f32[2]{0:T(128)S(1)} %get-tuple-element.209, ...), channel_id=1, replica_groups=mesh['gx_0'=2,'gx_1'=2,'gy'=4,'gz_0'=8,'gz_1'=8] {'gz_0'}, use_global_device_ids=true, to_apply=%region_31.32 | all-reduce | flops 10 | bytes 80 | tf_op jit(solution)/shard_map/psum | solution.py:36
  308.4 20.3 %all-reduce.7 = (f32[2]{0:T(128)S(1)}, f32[2]{0:T(128)S(1)}, f32[2]{0:T(128)S(1)}, f32[2]{0:T(128)S(1)}, f32[2]{0:T(128)S(1)}) all-reduce(f32[2]{0:T(128)S(1)} %get-tuple-element.198, f32[2]{0:T(128)S(1)} %get-tuple-element.199, f32[2]{0:T(128)S(1)} %get-tuple-element.200, ...), channel_id=1, replica_groups=mesh['gx_0'=2,'gx_1'=2,'gy'=4,'gz_0'=8,'gz_1'=8] {'gz_1'}, use_global_device_ids=true, to_apply=%region_32.33 | all-reduce | flops 10 | bytes 80 | tf_op jit(solution)/shard_map/psum | solution.py:36
  (147 shorter events, 88.8 us)
Async XLA Ops:
  9.8 7.0 %collective-permute-start = (f32[5,1,2,2,128]{4,3,2,1,0:T(2,128)S(1)}, f32[5,1,2,2,128]{4,3,2,1,0:T(2,128)S(1)}, u32[]{:S(2)}, u32[]{:S(2)}) collective-permute-start(f32[5,1,2,2,128]{4,3,2,1,0:T(2,128)S(1)} %pad_maximum_fusion.9), channel_id=1, source_target_pairs={{0,256},{256,512},{512,768},{768,0},{1,257},{257,513},{513,769},{7... | collective-permute-start | bytes 30728 | tf_op jit(solution)/shard_map/ppermute | solution.py:25
  11.7 15.7 %collective-permute-start.1 = (f32[5,1,2,2,128]{4,3,2,1,0:T(2,128)S(1)}, f32[5,1,2,2,128]{4,3,2,1,0:T(2,128)S(1)}, u32[]{:S(2)}, u32[]{:S(2)}) collective-permute-start(f32[5,1,2,2,128]{4,3,2,1,0:T(2,128)S(1)} %pad_maximum_fusion.9), channel_id=1, source_target_pairs={{256,0},{512,256},{768,512},{0,768},{257,1},{513,257},{769,513},{1... | collective-permute-start | bytes 30728 | tf_op jit(solution)/shard_map/ppermute | solution.py:27
  28.1 8.1 %collective-permute-start.2 = (f32[5,3,1,2,128]{4,3,2,1,0:T(2,128)S(1)}, f32[5,3,1,2,128]{4,3,2,1,0:T(2,128)S(1)}, u32[]{:S(2)}, u32[]{:S(2)}) collective-permute-start(f32[5,3,1,2,128]{4,3,2,1,0:T(2,128)S(1)} %get-tuple-element.254), channel_id=1, source_target_pairs={{0,64},{64,128},{128,192},{192,0},{1,65},{65,129},{129,193},{193,1... | collective-permute-start | bytes 46088 | tf_op jit(solution)/shard_map/ppermute | solution.py:25
  30.0 7.5 %collective-permute-start.3 = (f32[5,3,1,2,128]{4,3,2,1,0:T(2,128)S(1)}, f32[5,3,1,2,128]{4,3,2,1,0:T(2,128)S(1)}, u32[]{:S(2)}, u32[]{:S(2)}) collective-permute-start(f32[5,3,1,2,128]{4,3,2,1,0:T(2,128)S(1)} %get-tuple-element.255), channel_id=1, source_target_pairs={{64,0},{128,64},{192,128},{0,192},{65,1},{129,65},{193,129},{1,193... | collective-permute-start | bytes 46088 | tf_op jit(solution)/shard_map/ppermute | solution.py:27
  38.3 13.9 %collective-permute-start.4 = (f32[5,3,4,1,128]{4,3,2,1,0:T(1,128)S(1)}, f32[5,3,4,1,128]{4,3,2,1,0:T(1,128)S(1)}, u32[]{:S(2)}, u32[]{:S(2)}) collective-permute-start(f32[5,3,4,1,128]{4,3,2,1,0:T(1,128)S(1)} %get-tuple-element.252), channel_id=1, source_target_pairs={{0,1},{1,2},{2,3},{3,4},{4,5},{5,6},{6,7},{7,8},{8,9},{9,10},{10,1... | collective-permute-start | bytes 92168 | tf_op jit(solution)/shard_map/ppermute | solution.py:25
  40.2 12.7 %collective-permute-start.5 = (f32[5,3,4,1,128]{4,3,2,1,0:T(1,128)S(1)}, f32[5,3,4,1,128]{4,3,2,1,0:T(1,128)S(1)}, u32[]{:S(2)}, u32[]{:S(2)}) collective-permute-start(f32[5,3,4,1,128]{4,3,2,1,0:T(1,128)S(1)} %get-tuple-element.253), channel_id=1, source_target_pairs={{1,0},{2,1},{3,2},{4,3},{5,4},{6,5},{7,6},{8,7},{9,8},{10,9},{11,1... | collective-permute-start | bytes 92168 | tf_op jit(solution)/shard_map/ppermute | solution.py:27
  147.1 5.6 %collective-permute-start.6 = (f32[2,1,2,2,128]{4,0,3,2,1:T(2,128)S(1)}, f32[2,1,2,2,128]{4,0,3,2,1:T(2,128)S(1)}, u32[]{:S(2)}, u32[]{:S(2)}) collective-permute-start(f32[2,1,2,2,128]{4,0,3,2,1:T(2,128)S(1)} %bitcast.143), channel_id=1, source_target_pairs={{0,256},{256,512},{512,768},{768,0},{1,257},{257,513},{513,769},{7... | collective-permute-start | bytes 12296 | tf_op jit(solution)/shard_map/ppermute | solution.py:25
  149.0 5.0 %collective-permute-start.7 = (f32[2,1,2,2,128]{4,0,3,2,1:T(2,128)S(1)}, f32[2,1,2,2,128]{4,0,3,2,1:T(2,128)S(1)}, u32[]{:S(2)}, u32[]{:S(2)}) collective-permute-start(f32[2,1,2,2,128]{4,0,3,2,1:T(2,128)S(1)} %bitcast.144), channel_id=1, source_target_pairs={{256,0},{512,256},{768,512},{0,768},{257,1},{513,257},{769,513},{1... | collective-permute-start | bytes 12296 | tf_op jit(solution)/shard_map/ppermute | solution.py:27
  154.0 8.0 %collective-permute-start.8 = (f32[2,3,1,2,128]{4,0,3,2,1:T(2,128)S(1)}, f32[2,3,1,2,128]{4,0,3,2,1:T(2,128)S(1)}, u32[]{:S(2)}, u32[]{:S(2)}) collective-permute-start(f32[2,3,1,2,128]{4,0,3,2,1:T(2,128)S(1)} %get-tuple-element.262), channel_id=1, source_target_pairs={{0,64},{64,128},{128,192},{192,0},{1,65},{65,129},{129,193},{193,1... | collective-permute-start | bytes 18440 | tf_op jit(solution)/shard_map/ppermute | solution.py:25
  155.9 7.6 %collective-permute-start.9 = (f32[2,3,1,2,128]{4,0,3,2,1:T(2,128)S(1)}, f32[2,3,1,2,128]{4,0,3,2,1:T(2,128)S(1)}, u32[]{:S(2)}, u32[]{:S(2)}) collective-permute-start(f32[2,3,1,2,128]{4,0,3,2,1:T(2,128)S(1)} %get-tuple-element.263), channel_id=1, source_target_pairs={{64,0},{128,64},{192,128},{0,192},{65,1},{129,65},{193,129},{1,193... | collective-permute-start | bytes 18440 | tf_op jit(solution)/shard_map/ppermute | solution.py:27
  163.6 9.4 %collective-permute-start.10 = (f32[2,3,4,1,128]{4,0,3,2,1:T(2,128)S(1)}, f32[2,3,4,1,128]{4,0,3,2,1:T(2,128)S(1)}, u32[]{:S(2)}, u32[]{:S(2)}) collective-permute-start(f32[2,3,4,1,128]{4,0,3,2,1:T(2,128)S(1)} %get-tuple-element.258), channel_id=1, source_target_pairs={{0,1},{1,2},{2,3},{3,4},{4,5},{5,6},{6,7},{7,8},{8,9},{9,10},{10,1... | collective-permute-start | bytes 36872 | tf_op jit(solution)/shard_map/ppermute | solution.py:25
  165.5 8.6 %collective-permute-start.11 = (f32[2,3,4,1,128]{4,0,3,2,1:T(2,128)S(1)}, f32[2,3,4,1,128]{4,0,3,2,1:T(2,128)S(1)}, u32[]{:S(2)}, u32[]{:S(2)}) collective-permute-start(f32[2,3,4,1,128]{4,0,3,2,1:T(2,128)S(1)} %get-tuple-element.259), channel_id=1, source_target_pairs={{1,0},{2,1},{3,2},{4,3},{5,4},{6,5},{7,6},{8,7},{9,8},{10,9},{11,1... | collective-permute-start | bytes 36872 | tf_op jit(solution)/shard_map/ppermute | solution.py:27
  238.0 5.6 %collective-permute-start.12 = (f32[2,1,2,2,128]{4,0,3,2,1:T(2,128)S(1)}, f32[2,1,2,2,128]{4,0,3,2,1:T(2,128)S(1)}, u32[]{:S(2)}, u32[]{:S(2)}) collective-permute-start(f32[2,1,2,2,128]{4,0,3,2,1:T(2,128)S(1)} %bitcast.138), channel_id=1, source_target_pairs={{0,256},{256,512},{512,768},{768,0},{1,257},{257,513},{513,769},{7... | collective-permute-start | bytes 12296 | tf_op jit(solution)/shard_map/ppermute | solution.py:25
  239.9 5.0 %collective-permute-start.13 = (f32[2,1,2,2,128]{4,0,3,2,1:T(2,128)S(1)}, f32[2,1,2,2,128]{4,0,3,2,1:T(2,128)S(1)}, u32[]{:S(2)}, u32[]{:S(2)}) collective-permute-start(f32[2,1,2,2,128]{4,0,3,2,1:T(2,128)S(1)} %bitcast.139), channel_id=1, source_target_pairs={{256,0},{512,256},{768,512},{0,768},{257,1},{513,257},{769,513},{1... | collective-permute-start | bytes 12296 | tf_op jit(solution)/shard_map/ppermute | solution.py:27
  244.9 8.0 %collective-permute-start.14 = (f32[2,3,1,2,128]{4,0,3,2,1:T(2,128)S(1)}, f32[2,3,1,2,128]{4,0,3,2,1:T(2,128)S(1)}, u32[]{:S(2)}, u32[]{:S(2)}) collective-permute-start(f32[2,3,1,2,128]{4,0,3,2,1:T(2,128)S(1)} %get-tuple-element.260), channel_id=1, source_target_pairs={{0,64},{64,128},{128,192},{192,0},{1,65},{65,129},{129,193},{193,1... | collective-permute-start | bytes 18440 | tf_op jit(solution)/shard_map/ppermute | solution.py:25
  246.8 7.6 %collective-permute-start.15 = (f32[2,3,1,2,128]{4,0,3,2,1:T(2,128)S(1)}, f32[2,3,1,2,128]{4,0,3,2,1:T(2,128)S(1)}, u32[]{:S(2)}, u32[]{:S(2)}) collective-permute-start(f32[2,3,1,2,128]{4,0,3,2,1:T(2,128)S(1)} %get-tuple-element.261), channel_id=1, source_target_pairs={{64,0},{128,64},{192,128},{0,192},{65,1},{129,65},{193,129},{1,193... | collective-permute-start | bytes 18440 | tf_op jit(solution)/shard_map/ppermute | solution.py:27
  254.5 9.4 %collective-permute-start.16 = (f32[2,3,4,1,128]{4,0,3,2,1:T(2,128)S(1)}, f32[2,3,4,1,128]{4,0,3,2,1:T(2,128)S(1)}, u32[]{:S(2)}, u32[]{:S(2)}) collective-permute-start(f32[2,3,4,1,128]{4,0,3,2,1:T(2,128)S(1)} %get-tuple-element.256), channel_id=1, source_target_pairs={{0,1},{1,2},{2,3},{3,4},{4,5},{5,6},{6,7},{7,8},{8,9},{9,10},{10,1... | collective-permute-start | bytes 36872 | tf_op jit(solution)/shard_map/ppermute | solution.py:25
  256.4 8.6 %collective-permute-start.17 = (f32[2,3,4,1,128]{4,0,3,2,1:T(2,128)S(1)}, f32[2,3,4,1,128]{4,0,3,2,1:T(2,128)S(1)}, u32[]{:S(2)}, u32[]{:S(2)}) collective-permute-start(f32[2,3,4,1,128]{4,0,3,2,1:T(2,128)S(1)} %get-tuple-element.257), channel_id=1, source_target_pairs={{1,0},{2,1},{3,2},{4,3},{5,4},{6,5},{7,6},{8,7},{9,8},{10,9},{11,1... | collective-permute-start | bytes 36872 | tf_op jit(solution)/shard_map/ppermute | solution.py:27
where the time goes:
time: 333 us; the launch traced here: 332 us
  blocking collectives  164 us (49%)
  starting transfers between devices  72.1 us (22%)
  other arithmetic  34 us (10%)
  matrix products  25 us (8%)
  waiting for transfers between devices  20.7 us (6%)
  local copies, waits for them, and re-layouts  13.7 us (4%)
    psum x15, blocking collectives, over_axes(): shard = lax.psum(shard, axis)  164 us
    ppermute x9, starting transfers between devices, extended(): lax.ppermute(head, axis, [((i + 1) % count, i) for i in range(count)])  54.8 us
    dot_general x3, matrix products, apply_padded(): jnp.einsum('tsij,ctsj->cti', blocks, values, precision=lax.Precision.HIGH...  25 us
    ppermute x9, waiting for transfers between devices, extended(): lax.ppermute(head, axis, [((i + 1) % count, i) for i in range(count)])  20.7 us
    dynamic_update_slice x4, other arithmetic, per_device(): lax.map(build_tile, (own_pos, own_shield, row_index, shifts, listed, itse...  17.9 us
    ppermute x9, starting transfers between devices, extended(): lax.ppermute(tail, axis, [(i, (i + 1) % count) for i in range(count)])  17.3 us
  transfers between devices with their start and end apart: 18, of which 9 were waited for; matrix products, arithmetic and copies ran while one was open for 1% of the time, Pallas kernels for 0%

commit v1 on v0

v1 whole, which is shorter than its diff:
```python
import functools

import jax
import jax.numpy as jnp
from jax import lax
from jax.experimental import pallas as pl
from jax.experimental.pallas import tpu as pltpu
from jax.sharding import Mesh
from jax.sharding import PartitionSpec as P

GX = ("gx_0", "gx_1")
GZ = ("gz_0", "gz_1")
PLANE = ("gx_0", "gx_1", "gy")
GROUP_ONE = ("gx_0", "gx_1", "gz_1")
GROUP_TWO = ("gy", "gz_0")

CELL_EDGE = 11.0
CUTOFF = 10.0
COULOMB = 14.4
FAR = 1.0e4
ATOMS = 128
SLOTS = 27
FIELDS = 4
SHIFTS = (200.0, 100.0, 20.0)
DISPLACED = tuple((a, b, c) for a in (-1, 0, 1) for b in (-1, 0, 1) for c in (-1, 0, 1))
VMEM = pltpu.VMEM
F32 = jnp.float32


def call(body, outs, scratch=()):
    return pl.pallas_call(
        body,
        out_shape=tuple(jax.ShapeDtypeStruct(s, F32) for s in outs),
        out_specs=tuple(pl.BlockSpec(memory_space=VMEM) for _ in outs),
        scratch_shapes=list(scratch),
        compiler_params=pltpu.CompilerParams(vmem_limit_bytes=48 * 2**20),
    )


def vmem():
    return pl.BlockSpec(memory_space=VMEM)


def run(body, outs, args, specs=None, scratch=()):
    specs = specs or [vmem() for _ in args]
    return pl.pallas_call(
        body,
        out_shape=tuple(jax.ShapeDtypeStruct(s, F32) for s in outs),
        in_specs=specs,
        out_specs=tuple(vmem() for _ in outs),
        scratch_shapes=list(scratch),
        compiler_params=pltpu.CompilerParams(vmem_limit_bytes=48 * 2**20),
    )(*args)


def pack_body(offsets, type_ids, own, head, tail):
    for c in range(2):
        for b in range(2):
            row = (c * 2 + b) * FIELDS
            for axis in range(3):
                local = 0.0 if axis == 0 else CELL_EDGE * (b if axis == 1 else c)
                own[row + axis : row + axis + 1, :] = offsets[axis, 0, b, c : c + 1, :] + local
            own[row + 3 : row + 4, :] = type_ids[0, b, c : c + 1, :].astype(F32)
    head[...] = own[0:8, :]
    tail[...] = own[8:16, :]


def lookup(kinds, table):
    return jnp.where(kinds == 0.0, table[0], table[1])


def shield_of(kinds, gamma):
    value = lookup(kinds, gamma)
    return 1.0 / (value * jnp.sqrt(value))


def own_body(own, neighbours, gamma, columns, penalty):
    for b in range(2):
        for c in range(2):
            tile = b * 2 + c
            for field in range(FIELDS):
                row = (c * 2 + b) * FIELDS + field
                values = own[row : row + 1, :]
                if field == 3:
                    values = shield_of(values, gamma)
                columns[tile, field] = jnp.broadcast_to(values, (ATOMS, ATOMS)).T
            listed = neighbours[0, b, c : c + 1, :]
            slot = lax.broadcasted_iota(jnp.int32, (SLOTS, SLOTS), 0)
            one = jnp.where(slot >= 9, 1, 0) + jnp.where(slot >= 18, 1, 0)
            rest = slot - 9 * one
            two = jnp.where(rest >= 3, 1, 0) + jnp.where(rest >= 6, 1, 0)
            three = rest - 3 * two
            index = one * 16 + (two + b) * 4 + three + c
            found = jnp.max(jnp.where(listed == index, 1.0, 0.0), axis=1, keepdims=True)
            penalty[tile] = jnp.broadcast_to(jnp.where(found > 0.0, 0.0, FAR), (SLOTS, ATOMS))


def plane_position():
    first = lax.axis_index("gx_0") * 2 + lax.axis_index("gx_1")
    return first, lax.axis_index("gy")


def columns_of_plane():
    first, second = plane_position()
    for ix in range(3):
        for iy in range(4):
            step = -1 if iy == 0 else (1 if iy == 3 else 0)
            peer = ((first + ix + 3) % 4) * 4 + (second + step + 4) % 4
            yield ix, iy, peer, (iy + 1) % 2, step


def row_sums(acc):
    return jnp.sum(acc.T, axis=0, keepdims=True)


def build_body(
    received, columns, penalty, chi, eta, gamma, blocks, out, head, tail, near, acc
):
    for ix, iy, peer, b, step in columns_of_plane():
        for iz in range(4):
            p = (ix * 4 + iy) * 4 + iz
            row = (iz * 2 + b) * FIELDS
            cell = (received[peer, row + k : row + k + 1, :] for k in range(FIELDS))
            x, y, z, kinds = (jnp.broadcast_to(v, (8, ATOMS)) for v in cell)
            near[0, p] = x + CELL_EDGE * (ix - 1)
            near[1, p] = y + CELL_EDGE * 2 * step
            near[2, p] = z + (-2 * CELL_EDGE if iz == 0 else (2 * CELL_EDGE if iz == 3 else 0.0))
            near[3, p] = shield_of(kinds, gamma)
            near[4, p] = lookup(kinds, chi)

    half_rows = ATOMS // 2
    groups = half_rows // 8
    lane = lax.broadcasted_iota(jnp.int32, (8, ATOMS), 1)
    sub = lax.broadcasted_iota(jnp.int32, (8, ATOMS), 0)
    ratio = COULOMB / CUTOFF**7

    def half_tile(step, carry):
        tile = step // 2
        start = (step % 2) * half_rows
        base = 16 + (tile // 2 + 1) * 4 + tile % 2 + 1
        sums_s = [jnp.zeros((8, ATOMS), F32) for _ in range(groups)]
        sums_t = [jnp.zeros((8, ATOMS), F32) for _ in range(groups)]
        for d, (da, db, dc) in enumerate(DISPLACED):
            p = base + da * 16 + db * 4 + dc
            away = penalty[tile, d : d + 1, :]
            xj = near[0, p] + away
            yj, zj, sj, cj = near[1, p], near[2, p], near[3, p], near[4, p]
            for g in range(groups):
                rows = pl.ds(pl.multiple_of(start + g * 8, 8), 8)
                dx = xj - columns[tile, 0, rows, :]
                dy = yj - columns[tile, 1, rows, :]
                dz = zj - columns[tile, 2, rows, :]
                r2 = dx * dx + dy * dy + dz * dz
                r = r2 * lax.rsqrt(r2)
                x = r2 * r + columns[tile, 3, rows, :] * sj
                inverse = jnp.exp2(jnp.log(x) * (-1.0 / (3.0 * 0.6931471805599453)))
                w = jnp.maximum(CUTOFF - r, 0.0)
                w2 = w * w
                taper = (w2 * w2) * (
                    35.0e3 * ratio + w * (-84.0e2 * ratio + w * (70.0e1 * ratio + w * (-20.0 * ratio)))
                )
                value = taper * inverse
                if d == 13:
                    value = jnp.where(lane == sub + (start + g * 8), 0.0, value)
                blocks[tile, d, rows, :] = value
                sums_t[g] = sums_t[g] + value
                sums_s[g] = sums_s[g] + value * cj
        for g in range(groups):
            rows = pl.ds(pl.multiple_of(start + g * 8, 8), 8)
            acc[tile, 0, rows, :] = sums_s[g]
            acc[tile, 1, rows, :] = sums_t[g]
        return carry

    lax.fori_loop(0, 8, half_tile, 0)
    first, second = plane_position()
    me = first * 4 + second
    for c in range(2):
        for b in range(2):
            tile = b * 2 + c
            kinds = received[me, (((c + 1) * 2 + b) * FIELDS + 3) : (((c + 1) * 2 + b) * FIELDS + 4), :]
            shifted = lookup(kinds, eta) - SHIFTS[0]
            row = (c * 2 + b) * 2
            out[row : row + 1, :] = -(shifted * lookup(kinds, chi) + row_sums(acc[tile, 0]))
            out[row + 1 : row + 2, :] = -(shifted + row_sums(acc[tile, 1]))
    head[...] = out[0:4, :]
    tail[...] = out[4:8, :]


def image_rows(received, blocks, near, acc):
    for ix, iy, peer, b, step in columns_of_plane():
        for iz in range(4):
            p = (ix * 4 + iy) * 4 + iz
            for system in range(2):
                row = (iz * 2 + b) * 2 + system
                near[system, p] = jnp.broadcast_to(received[peer, row : row + 1, :], (8, ATOMS))
    half_rows = ATOMS // 2
    groups = half_rows // 8

    def half_tile(step, carry):
        tile = step // 2
        start = (step % 2) * half_rows
        base = 16 + (tile // 2 + 1) * 4 + tile % 2 + 1
        sums_s = [jnp.zeros((8, ATOMS), F32) for _ in range(groups)]
        sums_t = [jnp.zeros((8, ATOMS), F32) for _ in range(groups)]
        for d, (da, db, dc) in enumerate(DISPLACED):
            p = base + da * 16 + db * 4 + dc
            vs, vt = near[0, p], near[1, p]
            for g in range(groups):
                rows = pl.ds(pl.multiple_of(start + g * 8, 8), 8)
                value = blocks[tile, d, rows, :]
                sums_s[g] = sums_s[g] + value * vs
                sums_t[g] = sums_t[g] + value * vt
        for g in range(groups):
            rows = pl.ds(pl.multiple_of(start + g * 8, 8), 8)
            acc[tile, 0, rows, :] = sums_s[g]
            acc[tile, 1, rows, :] = sums_t[g]
        return carry

    lax.fori_loop(0, 8, half_tile, 0)


def next_vector(fields, eta, vector, acc, out, shift):
    for c in range(2):
        for b in range(2):
            tile = b * 2 + c
            row = (c * 2 + b) * FIELDS + 3
            shifted = lookup(fields[row : row + 1, :], eta) - shift
            for system in range(2):
                line = (c * 2 + b) * 2 + system
                out[line : line + 1, :] = shifted * vector[line : line + 1, :] + row_sums(
                    acc[tile, system]
                )


def second_body(received, blocks, fields, vector, eta, out, head, tail, near, acc):
    image_rows(received, blocks, near, acc)
    next_vector(fields, eta, vector, acc, out, SHIFTS[1])
    head[...] = out[0:4, :]
    tail[...] = out[4:8, :]


def source_rows(fields, chi):
    rows = []
    for cell in range(4):
        kinds = fields[cell * FIELDS + 3 : cell * FIELDS + 4, :]
        rows.append(-lookup(kinds, chi))
        rows.append(jnp.full((1, ATOMS), -1.0, F32))
    return jnp.concatenate(rows, axis=0)


def third_body(received, blocks, fields, w1, w2, chi, eta, out, sums, near, acc, moments):
    image_rows(received, blocks, near, acc)
    next_vector(fields, eta, w2, acc, out, SHIFTS[2])
    v0, v1, v2, v3 = source_rows(fields, chi), w1[...], w2[...], out[...]
    moments[...] = jnp.zeros((ATOMS, ATOMS), F32)
    pairs = (v0 * v0, v0 * v1, v0 * v2, v1 * v1, v1 * v2, v2 * v2, v2 * v3, v0, v1, v2)
    for k, item in enumerate(pairs):
        moments[2 * k : 2 * k + 2, :] = (item[0:2] + item[2:4]) + (item[4:6] + item[6:8])
    sums[...] = row_sums(moments[...])


def last_body(received, fields, w1, w2, w3, chi, charges, residuals):
    total = jnp.sum(received[...], axis=0)
    spread = jnp.broadcast_to(total, (ATOMS, ATOMS)).T
    g00, g01, g02, g11, g12, g22, g23, s0, s1, s2 = (spread[2 * k : 2 * k + 2, :] for k in range(10))
    shift0, shift1, shift2 = SHIFTS
    a00 = g01 + shift0 * g00
    a01 = g11 + shift0 * g01
    a02 = g12 + shift0 * g02
    a11 = g12 + shift1 * g11
    a12 = g22 + shift1 * g12
    a22 = g23 + shift2 * g22
    l10 = a01 / a00
    l20 = a02 / a00
    b11 = a11 - l10 * a01
    b12 = a12 - l10 * a02
    b22 = a22 - l20 * a02
    l21 = b12 / b11
    pivot = b22 - l21 * b12
    y1 = g01 - l10 * g00
    y2 = g02 - l20 * g00 - l21 * y1
    c2 = y2 / pivot
    c1 = (y1 - b12 * c2) / b11
    c0 = (g00 - a01 * c1 - a02 * c2) / a00
    level = c0 * s0 + c1 * s1 + c2 * s2
    level = level[0:1] / level[1:2]

    def every(value):
        return jnp.concatenate([value] * 4, axis=0)

    v0, v1, v2, v3 = source_rows(fields, chi), w1[...], w2[...], w3[...]
    solution_rows = every(c0) * v0 + every(c1) * v1 + every(c2) * v2
    residual_rows = (
        every(1.0 - shift0 * c0) * v0
        - every(c0 + shift1 * c1) * v1
        - every(c1 + shift2 * c2) * v2
        - every(c2) * v3
    )
    for c in range(2):
        for b in range(2):
            row = (c * 2 + b) * 2
            charges[0, b, c : c + 1, :] = 1000.0 * (
                solution_rows[row : row + 1] - level * solution_rows[row + 1 : row + 2]
            )
            for system in range(2):
                residuals[system, 0, b, c : c + 1, :] = residual_rows[row + system : row + system + 1]


def surrounded(own, head, tail):
    count = lax.axis_size(GZ)
    below = lax.ppermute(tail, GZ, [(i, (i + 1) % count) for i in range(count)])
    above = lax.ppermute(head, GZ, [((i + 1) % count, i) for i in range(count)])
    block = jnp.concatenate([below, own, above], axis=0)
    return lax.all_to_all(
        jnp.broadcast_to(block[None], (16,) + block.shape), PLANE, 0, 0, tiled=True
    )


def shared(row, axes):
    return lax.all_to_all(
        jnp.broadcast_to(row[None], (lax.axis_size(axes),) + row.shape), axes, 0, 0, tiled=True
    )


def per_device(offsets, type_ids, neighbours, type_chi, type_eta, type_gamma):
    smem = pl.BlockSpec(memory_space=pltpu.SMEM)
    fields, head, tail = run(pack_body, [(16, ATOMS), (8, ATOMS), (8, ATOMS)], (offsets, type_ids))
    columns, penalty = run(
        own_body,
        [(4, FIELDS, ATOMS, ATOMS), (4, SLOTS, ATOMS)],
        (fields, neighbours, type_gamma),
        [vmem(), vmem(), smem],
    )
    received = surrounded(fields, head, tail)
    matrix = (4, SLOTS, ATOMS, ATOMS)
    accumulate = VMEM((4, 2, ATOMS, ATOMS), F32)
    vectors = [(8, ATOMS), (4, ATOMS), (4, ATOMS)]
    blocks, w1, head, tail = run(
        build_body,
        [matrix] + vectors,
        (received, columns, penalty, type_chi, type_eta, type_gamma),
        [vmem(), vmem(), vmem(), smem, smem, smem],
        [VMEM((5, 48, 8, ATOMS), F32), accumulate],
    )
    near = VMEM((2, 48, 8, ATOMS), F32)
    received = surrounded(w1, head, tail)
    w2, head, tail = run(
        second_body,
        vectors,
        (received, blocks, fields, w1, type_eta),
        [vmem(), vmem(), vmem(), vmem(), smem],
        [near, accumulate],
    )
    received = surrounded(w2, head, tail)
    w3, sums = run(
        third_body,
        [(8, ATOMS), (1, ATOMS)],
        (received, blocks, fields, w1, w2, type_chi, type_eta),
        [vmem(), vmem(), vmem(), vmem(), vmem(), smem, smem],
        [near, accumulate, VMEM((ATOMS, ATOMS), F32)],
    )
    partial = jnp.sum(shared(sums, GROUP_ONE), axis=0)
    received = shared(partial, GROUP_TWO)
    return run(
        last_body,
        [(1, 2, 2, ATOMS), (2, 1, 2, 2, ATOMS)],
        (received, fields, w1, w2, w3, type_chi),
        [vmem(), vmem(), vmem(), vmem(), vmem(), smem],
    )


def solution(mesh):
    torus = Mesh(
        mesh.devices.reshape(2, 2, mesh.shape["gy"], 8, 8), ("gx_0", "gx_1", "gy", "gz_0", "gz_1")
    )
    in_specs = (
        P(None, GX, "gy", GZ, None),
        P(GX, "gy", GZ, None),
        P(GX, "gy", GZ, None),
        P(),
        P(),
        P(),
    )
    out_specs = (P(GX, "gy", GZ, None), P(None, GX, "gy", GZ, None))
    return jax.shard_map(
        per_device, mesh=torus, in_specs=in_specs, out_specs=out_specs, check_vma=False
    )
```

time: 333 us -> 144 us (0.43)
  the two profiles are of different devices: /device:TPU:16 before, /device:TPU:1 now
where the time goes in v1:
time: 144 us
  blocking collectives  54.1 us (38%)
  starting transfers between devices  49.5 us (34%)
  Pallas kernels  22.5 us (16%)
  waiting for transfers between devices  11.5 us (8%)
  local copies, waits for them, and re-layouts  5.45 us (4%)
    ppermute x3, starting transfers between devices, surrounded(): above = lax.ppermute(head, GZ, [((i + 1) % count, i) for i in range(count)])  32.6 us
    all_to_all x2, blocking collectives, shared(): lax.all_to_all(jnp.broadcast_to(row[None], (lax.axis_size(axes),) + row.s...  28.8 us
    all_to_all x2, blocking collectives, surrounded(): lax.all_to_all(jnp.broadcast_to(block[None], (16,) + block.shape), PLANE,...  25.3 us
    pallas_call x6, Pallas kernels, run(): pl.pallas_call(body, out_shape=tuple((jax.ShapeDtypeStruct(s, F32) for s...  22.5 us
    all_to_all x1, waiting for transfers between devices, surrounded(): lax.all_to_all(jnp.broadcast_to(block[None], (16,) + block.shape), PLANE,...  9.33 us
    all_to_all x1, starting transfers between devices, surrounded(): lax.all_to_all(jnp.broadcast_to(block[None], (16,) + block.shape), PLANE,...  9.1 us
    ppermute x3, starting transfers between devices, surrounded(): below = lax.ppermute(tail, GZ, [(i, (i + 1) % count) for i in range(count)])  7.78 us
    unnamed x16, local copies, waits for them, and re-layouts  4.66 us
  transfers between devices with their start and end apart: 7, of which 4 were waited for; matrix products, arithmetic and copies ran while one was open for 0% of the time, Pallas kernels for 1%

profile of v1, /device:TPU:1, one launch (start us, length us, event | category | flops | bytes accessed | tf_op | source)
XLA Modules:
  0.0 143.7 jit_solution(1574957102446293763)
XLA Ops:
  0.6 0.7 copy-done
  1.3 0.7 copy-done.6
  2.0 3.9 %collective-permute-start = (f32[8,128]{1,0:T(8,128)S(1)}, f32[8,128]{1,0:T(8,128)S(1)}, u32[]{:S(2)}, u32[]{:S(2)}) collective-permute-start(f32[8,128]{1,0:T(8,128)S(1)} %get-tuple-element.16), channel_id=1, source_target_pairs={{0,1},{1,2},{2,3},{3,4},{4,5},{5,6},{6,7},{7,8},{8,9},{9,10},{10,1... | collective-permute-start | bytes 12296 | tf_op jit(solution)/shard_map/ppermute | solution.py:311
  6.0 18.1 %collective-permute-start.1 = (f32[8,128]{1,0:T(8,128)S(1)}, f32[8,128]{1,0:T(8,128)S(1)}, u32[]{:S(2)}, u32[]{:S(2)}) collective-permute-start(f32[8,128]{1,0:T(8,128)S(1)} %get-tuple-element.18), channel_id=1, source_target_pairs={{1,0},{2,1},{3,2},{4,3},{5,4},{6,5},{7,6},{8,7},{9,8},{10,9},{11,1... | collective-permute-start | bytes 12296 | tf_op jit(solution)/shard_map/ppermute | solution.py:312
  24.1 0.7 collective-permute-done.1
  24.9 0.7 broadcast_in_dim.12
  25.6 9.1 %all-to-all-start = ((f32[16,32,128]{2,1,0:T(8,128)}), f32[16,32,128]{2,1,0:T(8,128)S(1)}, u32[]{:S(2)}, u32[]{:S(2)}) async-start(f32[16,32,128]{2,1,0:T(8,128)} %broadcast_in_dim.12), calls=%async_computation | async-start | bytes 524288 | tf_op jit(solution)/shard_map/all_to_all | solution.py:314
  35.4 0.7 copy-done.7
  36.0 0.9 shard_map.78
  37.0 9.3 %all-to-all-done.received = f32[16,32,128]{2,1,0:T(8,128)S(1)} async-done(((f32[16,32,128]{2,1,0:T(8,128)}), f32[16,32,128]{2,1,0:T(8,128)S(1)}, u32[]{:S(2)}, u32[]{:S(2)}) %all-to-all-start) | async-done | bytes 262176 | tf_op jit(solution)/shard_map/all_to_all | solution.py:314
  48.3 11.1 %shard_map.79 = (f32[4,27,128,128]{3,2,1,0:T(8,128)}, f32[8,128]{1,0:T(8,128)S(1)}, f32[4,128]{1,0:T(4,128)S(1)}, f32[4,128]{1,0:T(4,128)S(1)}) custom-call(f32[16,32,128]{2,1,0:T(8,128)S(1)} %all-to-all-done.received, f32[4,4,128,128]{3,2,1,0:T(8,128)S(1)} %get-tuple-element.19.columns, f32[4,27,128]{2,1,0:T(8,128)S(1)} %get-tuple-element.20.penalty, ...), custom_call_target="tpu_custom_call" | custom-call | tf_op jit(solution)/shard_map/pallas_call | solution.py:46
  59.3 1.9 %collective-permute-start.2 = (f32[4,128]{1,0:T(4,128)S(1)}, f32[4,128]{1,0:T(4,128)S(1)}, u32[]{:S(2)}, u32[]{:S(2)}) collective-permute-start(f32[4,128]{1,0:T(4,128)S(1)} %get-tuple-element.21), channel_id=1, source_target_pairs={{0,1},{1,2},{2,3},{3,4},{4,5},{5,6},{6,7},{7,8},{8,9},{9,10},{10,1... | collective-permute-start | bytes 6152 | tf_op jit(solution)/shard_map/ppermute | solution.py:311
  61.3 7.2 %collective-permute-start.3 = (f32[4,128]{1,0:T(4,128)S(1)}, f32[4,128]{1,0:T(4,128)S(1)}, u32[]{:S(2)}, u32[]{:S(2)}) collective-permute-start(f32[4,128]{1,0:T(4,128)S(1)} %get-tuple-element.23), channel_id=1, source_target_pairs={{1,0},{2,1},{3,2},{4,3},{5,4},{6,5},{7,6},{8,7},{9,8},{10,9},{11,1... | collective-permute-start | bytes 6152 | tf_op jit(solution)/shard_map/ppermute | solution.py:312
  68.5 0.7 collective-permute-done.3
  69.2 12.9 %all_to_all.25.received = f32[16,16,128]{2,1,0:T(8,128)S(1)} all-to-all(f32[16,16,128]{2,1,0:T(8,128)S(1)} %broadcast_in_dim.13), channel_id=1, replica_groups=mesh['gx_0'=2,'gx_1'=2,'gy'=4,'gz_0'=8,'gz_1'=8] {'gx_0','gx_1','gy'}, dimensions={0} | all-to-all | bytes 262144 | tf_op jit(solution)/shard_map/all_to_all | solution.py:314
  82.1 4.5 %shard_map.80 = (f32[8,128]{1,0:T(8,128)S(1)}, f32[4,128]{1,0:T(4,128)S(1)}, f32[4,128]{1,0:T(4,128)S(1)}) custom-call(f32[16,16,128]{2,1,0:T(8,128)S(1)} %all_to_all.25.received, f32[4,27,128,128]{3,2,1,0:T(8,128)} %get-tuple-element.24.blocks, f32[16,128]{1,0:T(8,128)S(1)} %get-tuple-element.17.own.fields, f32[8,128]{1,0:T(8,128)S(1)} %get-tuple-element.22.vector.w1, ...), custom_call_target="tpu_custom_call" | custom-call | tf_op jit(solution)/shard_map/pallas_call | solution.py:46
  86.7 1.9 %collective-permute-start.4 = (f32[4,128]{1,0:T(4,128)S(1)}, f32[4,128]{1,0:T(4,128)S(1)}, u32[]{:S(2)}, u32[]{:S(2)}) collective-permute-start(f32[4,128]{1,0:T(4,128)S(1)} %get-tuple-element.25), channel_id=1, source_target_pairs={{0,1},{1,2},{2,3},{3,4},{4,5},{5,6},{6,7},{7,8},{8,9},{9,10},{10,1... | collective-permute-start | bytes 6152 | tf_op jit(solution)/shard_map/ppermute | solution.py:311
  88.6 7.2 %collective-permute-start.5 = (f32[4,128]{1,0:T(4,128)S(1)}, f32[4,128]{1,0:T(4,128)S(1)}, u32[]{:S(2)}, u32[]{:S(2)}) collective-permute-start(f32[4,128]{1,0:T(4,128)S(1)} %get-tuple-element.27), channel_id=1, source_target_pairs={{1,0},{2,1},{3,2},{4,3},{5,4},{6,5},{7,6},{8,7},{9,8},{10,9},{11,1... | collective-permute-start | bytes 6152 | tf_op jit(solution)/shard_map/ppermute | solution.py:312
  95.8 0.7 collective-permute-done.5
  96.5 12.4 %all_to_all.26.received = f32[16,16,128]{2,1,0:T(8,128)S(1)} all-to-all(f32[16,16,128]{2,1,0:T(8,128)S(1)} %broadcast_in_dim.14), channel_id=1, replica_groups=mesh['gx_0'=2,'gx_1'=2,'gy'=4,'gz_0'=8,'gz_1'=8] {'gx_0','gx_1','gy'}, dimensions={0} | all-to-all | bytes 262144 | tf_op jit(solution)/shard_map/all_to_all | solution.py:314
  109.0 4.6 %shard_map.81 = (f32[8,128]{1,0:T(8,128)S(1)}, f32[1,128]{1,0:T(1,128)S(1)}) custom-call(f32[16,16,128]{2,1,0:T(8,128)S(1)} %all_to_all.26.received, f32[4,27,128,128]{3,2,1,0:T(8,128)} %get-tuple-element.24.blocks, f32[16,128]{1,0:T(8,128)S(1)} %get-tuple-element.17.own.fields, f32[8,128]{1,0:T(8,128)S(1)} %get-tuple-element.22.vector.w1, ...), custom_call_target="tpu_custom_call" | custom-call | tf_op jit(solution)/shard_map/pallas_call | solution.py:46
  113.6 10.0 %all_to_all.27 = f32[32,1,128]{2,1,0:T(1,128)S(1)} all-to-all(f32[32,1,128]{2,1,0:T(1,128)S(1)} %broadcast_in_dim.16), channel_id=1, replica_groups=mesh['gx_0'=2,'gx_1'=2,'gy'=4,'gz_0'=8,'gz_1'=8] {'gx_0','gx_1','gz_1'}, dimensions={0} | all-to-all | bytes 32768 | tf_op jit(solution)/shard_map/all_to_all | solution.py:320
  123.7 18.8 %all_to_all.28.received = f32[32,1,128]{2,1,0:T(1,128)S(1)} all-to-all(f32[32,1,128]{2,1,0:T(1,128)S(1)} %broadcast_in_dim.17), channel_id=1, replica_groups=mesh['gx_0'=2,'gx_1'=2,'gy'=4,'gz_0'=8,'gz_1'=8] {'gy','gz_0'}, dimensions={0} | all-to-all | bytes 32768 | tf_op jit(solution)/shard_map/all_to_all | solution.py:320
  142.4 1.3 shard_map.82
  (25 shorter events, 2.7 us)
Async XLA Ops:
  0.6 0.7 copy-start
  1.3 0.7 copy-start.6
  2.0 22.1 %collective-permute-start = (f32[8,128]{1,0:T(8,128)S(1)}, f32[8,128]{1,0:T(8,128)S(1)}, u32[]{:S(2)}, u32[]{:S(2)}) collective-permute-start(f32[8,128]{1,0:T(8,128)S(1)} %get-tuple-element.16), channel_id=1, source_target_pairs={{0,1},{1,2},{2,3},{3,4},{4,5},{5,6},{6,7},{7,8},{8,9},{9,10},{10,1... | collective-permute-start | bytes 12296 | tf_op jit(solution)/shard_map/ppermute | solution.py:311
  6.0 18.9 %collective-permute-start.1 = (f32[8,128]{1,0:T(8,128)S(1)}, f32[8,128]{1,0:T(8,128)S(1)}, u32[]{:S(2)}, u32[]{:S(2)}) collective-permute-start(f32[8,128]{1,0:T(8,128)S(1)} %get-tuple-element.18), channel_id=1, source_target_pairs={{1,0},{2,1},{3,2},{4,3},{5,4},{6,5},{7,6},{8,7},{9,8},{10,9},{11,1... | collective-permute-start | bytes 12296 | tf_op jit(solution)/shard_map/ppermute | solution.py:312
  25.6 20.7 %all-to-all-start = ((f32[16,32,128]{2,1,0:T(8,128)}), f32[16,32,128]{2,1,0:T(8,128)S(1)}, u32[]{:S(2)}, u32[]{:S(2)}) async-start(f32[16,32,128]{2,1,0:T(8,128)} %broadcast_in_dim.12), calls=%async_computation | async-start | bytes 524288 | tf_op jit(solution)/shard_map/all_to_all | solution.py:314
  34.7 0.7 copy-start.4
  35.4 0.7 copy-start.7
  46.3 0.7 copy-start.1
  47.0 0.7 copy-start.2
  47.6 0.7 copy-start.5
  59.3 9.2 %collective-permute-start.2 = (f32[4,128]{1,0:T(4,128)S(1)}, f32[4,128]{1,0:T(4,128)S(1)}, u32[]{:S(2)}, u32[]{:S(2)}) collective-permute-start(f32[4,128]{1,0:T(4,128)S(1)} %get-tuple-element.21), channel_id=1, source_target_pairs={{0,1},{1,2},{2,3},{3,4},{4,5},{5,6},{6,7},{7,8},{8,9},{9,10},{10,1... | collective-permute-start | bytes 6152 | tf_op jit(solution)/shard_map/ppermute | solution.py:311
  61.3 7.9 %collective-permute-start.3 = (f32[4,128]{1,0:T(4,128)S(1)}, f32[4,128]{1,0:T(4,128)S(1)}, u32[]{:S(2)}, u32[]{:S(2)}) collective-permute-start(f32[4,128]{1,0:T(4,128)S(1)} %get-tuple-element.23), channel_id=1, source_target_pairs={{1,0},{2,1},{3,2},{4,3},{5,4},{6,5},{7,6},{8,7},{9,8},{10,9},{11,1... | collective-permute-start | bytes 6152 | tf_op jit(solution)/shard_map/ppermute | solution.py:312
  82.1 60.3 %copy-start.3 = (f32[2]{0:T(128)S(1)}, f32[2]{0:T(128)}, u32[]{:S(2)}) copy-start(f32[2]{0:T(128)} %chi.5) | copy-start | bytes 28
  86.7 9.2 %collective-permute-start.4 = (f32[4,128]{1,0:T(4,128)S(1)}, f32[4,128]{1,0:T(4,128)S(1)}, u32[]{:S(2)}, u32[]{:S(2)}) collective-permute-start(f32[4,128]{1,0:T(4,128)S(1)} %get-tuple-element.25), channel_id=1, source_target_pairs={{0,1},{1,2},{2,3},{3,4},{4,5},{5,6},{6,7},{7,8},{8,9},{9,10},{10,1... | collective-permute-start | bytes 6152 | tf_op jit(solution)/shard_map/ppermute | solution.py:311
  88.6 7.9 %collective-permute-start.5 = (f32[4,128]{1,0:T(4,128)S(1)}, f32[4,128]{1,0:T(4,128)S(1)}, u32[]{:S(2)}, u32[]{:S(2)}) collective-permute-start(f32[4,128]{1,0:T(4,128)S(1)} %get-tuple-element.27), channel_id=1, source_target_pairs={{1,0},{2,1},{3,2},{4,3},{5,4},{6,5},{7,6},{8,7},{9,8},{10,9},{11,1... | collective-permute-start | bytes 6152 | tf_op jit(solution)/shard_map/ppermute | solution.py:312

commit v2 on v1

v2 whole, which is shorter than its diff:
```python
import functools

import jax
import jax.numpy as jnp
from jax import lax
from jax.experimental import pallas as pl
from jax.experimental.pallas import tpu as pltpu
from jax.sharding import Mesh
from jax.sharding import PartitionSpec as P

GX = ("gx_0", "gx_1")
GZ = ("gz_0", "gz_1")
PLANE = ("gx_0", "gx_1", "gy")
GROUP_ONE = ("gx_0", "gx_1", "gz_1")
GROUP_TWO = ("gy", "gz_0")

CELL_EDGE = 11.0
CUTOFF = 10.0
SCALE = 14.4 * 0.02 / CUTOFF**4
FAR = 1.0e4
ATOMS = 128
GROUPS = 8
FIELDS = 4
SHIFTS = (200.0, 100.0, 20.0)
INNER = tuple((ix, jy, k) for ix in range(3) for jy in range(3) for k in range(2))
OUTER = tuple((ix, jy) for ix in range(3) for jy in range(3))
VMEM = pltpu.VMEM
HBM = pltpu.HBM
F32 = jnp.float32


def run(body, outs, args, spaces=None, scratch=()):
    spaces = spaces or [VMEM] * len(args)
    held = [
        pltpu.with_memory_space_constraint(x, VMEM if space == VMEM else HBM)
        for x, space in zip(args, spaces)
    ]
    return pl.pallas_call(
        body,
        out_shape=tuple(VMEM(shape, F32) for shape in outs),
        in_specs=[pl.BlockSpec(memory_space=space) for space in spaces],
        out_specs=tuple(pl.BlockSpec(memory_space=VMEM) for _ in outs),
        scratch_shapes=list(scratch),
        compiler_params=pltpu.CompilerParams(vmem_limit_bytes=12 * 2**20),
    )(*held)


def pack_body(offsets_far, types_far, own, offsets, type_ids, one, two):
    first = pltpu.make_async_copy(offsets_far, offsets, one)
    second = pltpu.make_async_copy(types_far, type_ids, two)
    first.start()
    second.start()
    first.wait()
    second.wait()
    for c in range(2):
        for b in range(2):
            row = (c * 2 + b) * FIELDS
            for axis in range(3):
                local = 0.0 if axis == 0 else CELL_EDGE * (b if axis == 1 else c)
                own[row + axis : row + axis + 1, :] = offsets[axis, 0, b, c : c + 1, :] + local
            own[row + 3 : row + 4, :] = type_ids[0, b, c : c + 1, :].astype(F32)


def plane_columns():
    first = lax.axis_index("gx_0") * 2 + lax.axis_index("gx_1")
    second = lax.axis_index("gy")
    for ix in range(3):
        for iy in range(4):
            step = -1 if iy == 0 else (1 if iy == 3 else 0)
            peer = ((first + ix + 3) % 4) * 4 + (second + step + 4) % 4
            yield ix, iy, peer, (iy + 1) % 2, step


def faces_body(received, head, tail):
    for ix, iy, peer, b, step in plane_columns():
        for face, c in ((head, 0), (tail, 1)):
            row = (c * 2 + b) * FIELDS
            line = (ix * 4 + iy) * FIELDS
            face[line : line + 1, :] = received[peer, row : row + 1, :] + CELL_EDGE * (ix - 1)
            face[line + 1 : line + 2, :] = received[peer, row + 1 : row + 2, :] + CELL_EDGE * 2 * step
            face[line + 2 : line + 4, :] = received[peer, row + 2 : row + 4, :]


def choose(kinds, table, first):
    return jnp.where(kinds == 0.0, table[first : first + 1, :], table[first + 1 : first + 2, :])


def place(near, index, lines, table, lift):
    x, y, z, kinds = (jnp.broadcast_to(v, (8, ATOMS)) for v in lines)
    near[0, index] = x
    near[1, index] = y
    near[2, index] = z + lift
    near[3, index] = choose(kinds, table, 0)
    near[4, index] = choose(kinds, table, 2)


def row_sums(acc):
    return jnp.sum(acc.T, axis=0, keepdims=True)


def couple(near, columns, away, tile, start, p, line, blocks, slot, sums_s, sums_t, mask):
    xj = near[0, p] + away[tile, line : line + 1, :]
    yj, zj, sj, cj = near[1, p], near[2, p], near[3, p], near[4, p]
    for g in range(GROUPS):
        rows = pl.ds(pl.multiple_of(start + g * 8, 8), 8)
        dx = xj - columns[tile, 0, rows, :]
        dy = yj - columns[tile, 1, rows, :]
        dz = zj - columns[tile, 2, rows, :]
        r2 = dx * dx + dy * dy + dz * dz
        r = r2 * lax.rsqrt(r2)
        x = r2 * r + columns[tile, 3, rows, :] * sj
        inverse = jnp.exp2(lax.log2(x) * (-1.0 / 3.0))
        w = jnp.maximum(CUTOFF - r, 0.0)
        w2 = w * w
        value = (w2 * w2) * (((r + 5.0) * r + 20.0) * r + 50.0) * inverse
        if mask is not None:
            value = jnp.where(mask(g), 0.0, value)
        blocks[tile, slot, rows, :] = value
        sums_t[g] = sums_t[g] + value
        sums_s[g] = sums_s[g] + value * cj


def store(acc, tile, start, sums_s, sums_t):
    for g in range(GROUPS):
        rows = pl.ds(pl.multiple_of(start + g * 8, 8), 8)
        acc[tile, 0, rows, :] = sums_s[g]
        acc[tile, 1, rows, :] = sums_t[g]


def listed(entries, index):
    found = jnp.max(jnp.where(entries == index, 1.0, 0.0), axis=1, keepdims=True)
    return jnp.broadcast_to(jnp.where(found > 0.0, 0.0, FAR), (index.shape[0], ATOMS))


def split(number, by, parts):
    high = sum(jnp.where(number >= by * k, 1, 0) for k in range(1, parts))
    return high, number - by * high


def inner_body(
    received, own, neighbours, chi, eta, gamma, face,
    blocks, acc, columns, away_outer, table, face_out, near, away,
):
    for kind in range(2):
        value = jnp.full((1, ATOMS), gamma[kind], F32)
        table[kind : kind + 1, :] = 1.0 / (value * jnp.sqrt(value))
        table[2 + kind : 3 + kind, :] = jnp.full((1, ATOMS), chi[kind], F32)
        table[4 + kind : 5 + kind, :] = jnp.full((1, ATOMS), eta[kind], F32)
    face_out[...] = face[...]
    for b in range(2):
        for c in range(2):
            tile = b * 2 + c
            for field in range(FIELDS):
                row = (c * 2 + b) * FIELDS + field
                values = own[row : row + 1, :]
                if field == 3:
                    values = choose(values, table, 0)
                columns[tile, field] = jnp.broadcast_to(values, (ATOMS, ATOMS)).T
            entries = neighbours[0, b, c : c + 1, :]
            slot = lax.broadcasted_iota(jnp.int32, (18, 27), 0)
            ix, rest = split(slot, 6, 3)
            jy, k = split(rest, 2, 3)
            away[tile] = listed(entries, ix * 16 + (jy + b) * 4 + k + 1)
            slot = lax.broadcasted_iota(jnp.int32, (9, 27), 0)
            ix, jy = split(slot, 3, 3)
            away_outer[tile] = listed(entries, ix * 16 + (jy + b) * 4 + 3 * c)
    for ix, iy, peer, b, step in plane_columns():
        for k in range(2):
            row = (k * 2 + b) * FIELDS
            lines = [received[peer, row + f : row + f + 1, :] for f in range(FIELDS)]
            lines[0] = lines[0] + CELL_EDGE * (ix - 1)
            lines[1] = lines[1] + CELL_EDGE * 2 * step
            place(near, (ix * 4 + iy) * 2 + k, lines, table, 0.0)

    lane = lax.broadcasted_iota(jnp.int32, (8, ATOMS), 1)
    sub = lax.broadcasted_iota(jnp.int32, (8, ATOMS), 0)

    def half_tile(step, carry):
        tile = step // 2
        b, c = tile // 2, tile % 2
        start = (step % 2) * (GROUPS * 8)
        sums_s = [jnp.zeros((8, ATOMS), F32) for _ in range(GROUPS)]
        sums_t = [jnp.zeros((8, ATOMS), F32) for _ in range(GROUPS)]
        for slot, (ix, jy, k) in enumerate(INNER):
            mask = None
            if (ix, jy) == (1, 1):
                first = start + jnp.where(c == k, 0, 2 * ATOMS)
                mask = functools.partial(lambda at, g: lane == sub + (at + g * 8), first)
            p = (ix * 4 + jy + b) * 2 + k
            couple(near, columns, away, tile, start, p, slot, blocks, slot, sums_s, sums_t, mask)
        store(acc, tile, start, sums_s, sums_t)
        return carry

    lax.fori_loop(0, 8, half_tile, 0)


def outer_body(
    below, above, own, columns, away, table, partial,
    blocks, out, head, tail, near, acc,
):
    for ix in range(3):
        for iy in range(4):
            line = (ix * 4 + iy) * FIELDS
            for side, (ghost, lift) in enumerate(((below, -2 * CELL_EDGE), (above, 2 * CELL_EDGE))):
                lines = [ghost[line + f : line + f + 1, :] for f in range(FIELDS)]
                place(near, (ix * 4 + iy) * 2 + side, lines, table, lift)

    def half_tile(step, carry):
        tile = step // 2
        b, c = tile // 2, tile % 2
        start = (step % 2) * (GROUPS * 8)
        rows = [pl.ds(pl.multiple_of(start + g * 8, 8), 8) for g in range(GROUPS)]
        sums_s = [partial[tile, 0, r, :] for r in rows]
        sums_t = [partial[tile, 1, r, :] for r in rows]
        for slot, (ix, jy) in enumerate(OUTER):
            p = (ix * 4 + jy + b) * 2 + c
            couple(near, columns, away, tile, start, p, slot, blocks, slot, sums_s, sums_t, None)
        store(acc, tile, start, sums_s, sums_t)
        return carry

    lax.fori_loop(0, 8, half_tile, 0)
    source = source_rows(own, table)
    next_vector(own, table, source, acc, out, SHIFTS[0], (-SCALE, -SCALE))
    head[...] = out[0:4, :]
    tail[...] = out[4:8, :]


def image_rows(received, inner, outer, near, acc):
    for ix, iy, peer, b, step in plane_columns():
        for iz in range(4):
            for system in range(2):
                row = (iz * 2 + b) * 2 + system
                near[system, (ix * 4 + iy) * 4 + iz] = jnp.broadcast_to(
                    received[peer, row : row + 1, :], (8, ATOMS)
                )
    groups = ATOMS // 8

    def one_tile(tile, carry):
        b, c = tile // 2, tile % 2
        sums_s = [jnp.zeros((8, ATOMS), F32) for _ in range(groups)]
        sums_t = [jnp.zeros((8, ATOMS), F32) for _ in range(groups)]
        places = [((ix * 4 + jy + b) * 4 + k + 1, inner, n) for n, (ix, jy, k) in enumerate(INNER)]
        places += [((ix * 4 + jy + b) * 4 + 3 * c, outer, n) for n, (ix, jy) in enumerate(OUTER)]
        for p, blocks, slot in places:
            vs, vt = near[0, p], near[1, p]
            for g in range(groups):
                value = blocks[tile, slot, g * 8 : g * 8 + 8, :]
                sums_s[g] = sums_s[g] + value * vs
                sums_t[g] = sums_t[g] + value * vt
        for g in range(groups):
            acc[tile, 0, g * 8 : g * 8 + 8, :] = sums_s[g]
            acc[tile, 1, g * 8 : g * 8 + 8, :] = sums_t[g]
        return carry

    lax.fori_loop(0, 4, one_tile, 0)


def next_vector(own, table, vector, acc, out, shift, scales=(SCALE, SCALE)):
    for c in range(2):
        for b in range(2):
            tile = b * 2 + c
            kind = (c * 2 + b) * FIELDS + 3
            shifted = choose(own[kind : kind + 1, :], table, 4) - shift
            for system in range(2):
                line = (c * 2 + b) * 2 + system
                out[line : line + 1, :] = shifted * vector[line : line + 1, :] + scales[
                    system
                ] * row_sums(acc[tile, system])


def second_body(received, inner, outer, own, table, vector, out, head, tail, near, acc):
    image_rows(received, inner, outer, near, acc)
    next_vector(own, table, vector, acc, out, SHIFTS[1])
    head[...] = out[0:4, :]
    tail[...] = out[4:8, :]


def source_rows(own, table):
    rows = []
    for cell in range(4):
        kind = cell * FIELDS + 3
        rows.append(-choose(own[kind : kind + 1, :], table, 2))
        rows.append(jnp.full((1, ATOMS), -1.0, F32))
    return jnp.concatenate(rows, axis=0)


def third_body(received, inner, outer, own, table, w1, w2, out, sums, near, acc, moments):
    image_rows(received, inner, outer, near, acc)
    next_vector(own, table, w2, acc, out, SHIFTS[2])
    v0, v1, v2, v3 = source_rows(own, table), w1[...], w2[...], out[...]
    moments[...] = jnp.zeros((ATOMS, ATOMS), F32)
    pairs = (v0 * v0, v0 * v1, v0 * v2, v1 * v1, v1 * v2, v2 * v2, v2 * v3, v0, v1, v2)
    for k, item in enumerate(pairs):
        moments[2 * k : 2 * k + 2, :] = (item[0:2] + item[2:4]) + (item[4:6] + item[6:8])
    sums[...] = row_sums(moments[...])


def last_body(received, own, table, w1, w2, w3, charges, residuals):
    total = jnp.sum(received[...], axis=0)
    spread = jnp.broadcast_to(total, (ATOMS, ATOMS)).T
    g00, g01, g02, g11, g12, g22, g23, s0, s1, s2 = (spread[2 * k : 2 * k + 2, :] for k in range(10))
    shift0, shift1, shift2 = SHIFTS
    a00 = g01 + shift0 * g00
    a01 = g11 + shift0 * g01
    a02 = g12 + shift0 * g02
    a11 = g12 + shift1 * g11
    a12 = g22 + shift1 * g12
    a22 = g23 + shift2 * g22
    l10 = a01 / a00
    l20 = a02 / a00
    b11 = a11 - l10 * a01
    b12 = a12 - l10 * a02
    b22 = a22 - l20 * a02
    l21 = b12 / b11
    pivot = b22 - l21 * b12
    y1 = g01 - l10 * g00
    y2 = g02 - l20 * g00 - l21 * y1
    c2 = y2 / pivot
    c1 = (y1 - b12 * c2) / b11
    c0 = (g00 - a01 * c1 - a02 * c2) / a00
    level = c0 * s0 + c1 * s1 + c2 * s2
    level = level[0:1] / level[1:2]

    def every(value):
        return jnp.concatenate([value] * 4, axis=0)

    v0, v1, v2, v3 = source_rows(own, table), w1[...], w2[...], w3[...]
    solution_rows = every(c0) * v0 + every(c1) * v1 + every(c2) * v2
    residual_rows = (
        every(1.0 - shift0 * c0) * v0
        - every(c0 + shift1 * c1) * v1
        - every(c1 + shift2 * c2) * v2
        - every(c2) * v3
    )
    for c in range(2):
        for b in range(2):
            row = (c * 2 + b) * 2
            charges[0, b, c : c + 1, :] = 1000.0 * (
                solution_rows[row : row + 1] - level * solution_rows[row + 1 : row + 2]
            )
            for system in range(2):
                residuals[system, 0, b, c : c + 1, :] = residual_rows[row + system : row + system + 1]


def upward(tail):
    count = lax.axis_size(GZ)
    return lax.ppermute(tail, GZ, [(i, (i + 1) % count) for i in range(count)])


def downward(head):
    count = lax.axis_size(GZ)
    return lax.ppermute(head, GZ, [((i + 1) % count, i) for i in range(count)])


def shared(block, axes):
    count = lax.axis_size(axes)
    return lax.all_to_all(
        jnp.broadcast_to(block[None], (count,) + block.shape), axes, 0, 0, tiled=True
    )


def surrounded(own, head, tail):
    return shared(jnp.concatenate([upward(tail), own, downward(head)], axis=0), PLANE)


def per_device(offsets, type_ids, neighbours, type_chi, type_eta, type_gamma):
    smem = pltpu.SMEM
    (own,) = run(
        pack_body,
        [(16, ATOMS)],
        (offsets, type_ids),
        [HBM, HBM],
        [
            VMEM(offsets.shape, F32),
            VMEM(type_ids.shape, jnp.int32),
            pltpu.SemaphoreType.DMA,
            pltpu.SemaphoreType.DMA,
        ],
    )
    received = shared(own, PLANE)
    head, tail = run(faces_body, [(48, ATOMS), (48, ATOMS)], (received,))
    below = upward(tail)
    products = (4, 2, ATOMS, ATOMS)
    accumulate = VMEM(products, F32)
    inner, partial, columns, away, table, head = run(
        inner_body,
        [(4, 18, ATOMS, ATOMS), products, (4, FIELDS, ATOMS, ATOMS), (4, 9, ATOMS), (8, ATOMS), (48, ATOMS)],
        (received, own, neighbours, type_chi, type_eta, type_gamma, head),
        [VMEM, VMEM, VMEM, smem, smem, smem, VMEM],
        [VMEM((5, 24, 8, ATOMS), F32), VMEM((4, 18, ATOMS), F32)],
    )
    above = downward(head)
    vectors = [(8, ATOMS), (4, ATOMS), (4, ATOMS)]
    outer, w1, head, tail = run(
        outer_body,
        [(4, 9, ATOMS, ATOMS)] + vectors,
        (below, above, own, columns, away, table, partial),
        scratch=[VMEM((5, 24, 8, ATOMS), F32), accumulate],
    )
    near = VMEM((2, 48, 8, ATOMS), F32)
    received = surrounded(w1, head, tail)
    w2, head, tail = run(
        second_body, vectors, (received, inner, outer, own, table, w1), scratch=[near, accumulate]
    )
    received = surrounded(w2, head, tail)
    w3, sums = run(
        third_body,
        [(8, ATOMS), (1, ATOMS)],
        (received, inner, outer, own, table, w1, w2),
        scratch=[near, accumulate, VMEM((ATOMS, ATOMS), F32)],
    )
    half = jnp.sum(shared(sums, GROUP_ONE), axis=0)
    received = shared(half, GROUP_TWO)
    held = [pltpu.with_memory_space_constraint(x, VMEM) for x in (received, own, table, w1, w2, w3)]
    return pl.pallas_call(
        last_body,
        out_shape=(
            jax.ShapeDtypeStruct((1, 2, 2, ATOMS), F32),
            jax.ShapeDtypeStruct((2, 1, 2, 2, ATOMS), F32),
        ),
        in_specs=[pl.BlockSpec(memory_space=VMEM)] * 6,
        out_specs=(pl.BlockSpec(memory_space=VMEM),) * 2,
    )(*held)


def solution(mesh):
    torus = Mesh(
        mesh.devices.reshape(2, 2, mesh.shape["gy"], 8, 8), ("gx_0", "gx_1", "gy", "gz_0", "gz_1")
    )
    in_specs = (
        P(None, GX, "gy", GZ, None),
        P(GX, "gy", GZ, None),
        P(GX, "gy", GZ, None),
        P(),
        P(),
        P(),
    )
    out_specs = (P(GX, "gy", GZ, None), P(None, GX, "gy", GZ, None))
    return jax.shard_map(
        per_device, mesh=torus, in_specs=in_specs, out_specs=out_specs, check_vma=False
    )
```

time: 144 us -> 130 us (0.903)
  blocking collectives: 54.1 us -> 80.3 us
  starting transfers between devices: 49.5 us -> 31.9 us
  Pallas kernels: 22.5 us -> 13.2 us
  waiting for transfers between devices: 11.5 us -> 2.35 us
  local copies, waits for them, and re-layouts: 5.45 us -> 0.74 us
    all_to_all x4 -> x5, blocking collectives: 54.1 us -> 80.3 us  [shared(): lax.all_to_all(jnp.broadcast_to(block[None], (count,) + block.shape), axe...]
    all_to_all x1 -> x0, waiting for transfers between devices: 9.33 us -> none  [surrounded(): lax.all_to_all(jnp.broadcast_to(block[None], (16,) + block.shape), PLANE,...]
    pallas_call x6 -> x7, Pallas kernels: 22.5 us -> 13.2 us  [the longest x6 12.4 us: run(): pl.pallas_call(body, out_shape=tuple((VMEM(shape, F32) for shape in outs)...]
    all_to_all x1 -> x0, starting transfers between devices: 9.1 us -> none  [surrounded(): lax.all_to_all(jnp.broadcast_to(block[None], (16,) + block.shape), PLANE,...]
    ppermute x6, starting transfers between devices: 40.4 us -> 31.9 us  [the longest x3 26.1 us: downward(): return lax.ppermute(head, GZ, [((i + 1) % count, i) for i in range(count)])]
    unnamed x16 -> x2, local copies, waits for them, and re-layouts: 4.66 us -> 0.68 us
  transfers between devices with their start and end apart: 7 -> 6, of which waited for: 4 -> 3; matrix products, arithmetic and copies ran while one was open for 0% -> 0% of each run, Pallas kernels for 1% -> 5%
where the time goes in v2:
time: 130 us; the launch traced here: 129 us
  blocking collectives  80.3 us (62%)
  starting transfers between devices  31.9 us (25%)
  Pallas kernels  13.2 us (10%)
  waiting for transfers between devices  2.35 us (2%)
    all_to_all x5, blocking collectives, shared(): lax.all_to_all(jnp.broadcast_to(block[None], (count,) + block.shape), axe...  80.3 us
    ppermute x3, starting transfers between devices, downward(): return lax.ppermute(head, GZ, [((i + 1) % count, i) for i in range(count)])  26.1 us
    pallas_call x6, Pallas kernels, run(): pl.pallas_call(body, out_shape=tuple((VMEM(shape, F32) for shape in outs)...  12.4 us
    ppermute x3, starting transfers between devices, upward(): return lax.ppermute(tail, GZ, [(i, (i + 1) % count) for i in range(count)])  5.76 us
  transfers between devices with their start and end apart: 6, of which 3 were waited for; matrix products, arithmetic and copies ran while one was open for 0% of the time, Pallas kernels for 5%

profile of v2, /device:TPU:1, one launch (start us, length us, event | category | flops | bytes accessed | tf_op | source)
XLA Modules:
  0.0 129.2 jit_solution(11954524908336434782)
XLA Ops:
  0.6 0.7 shard_map.77.own
  1.4 25.8 %all_to_all.25.received = f32[16,16,128]{2,1,0:T(8,128)S(1)} all-to-all(f32[16,16,128]{2,1,0:T(8,128)S(1)} %broadcast_in_dim.12), channel_id=1, replica_groups=mesh['gx_0'=2,'gx_1'=2,'gy'=4,'gz_0'=8,'gz_1'=8] {'gx_0','gx_1','gy'}, dimensions={0} | all-to-all | bytes 262144 | tf_op jit(solution)/shard_map/all_to_all | solution.py:357
  27.2 1.9 %collective-permute-start = (f32[48,128]{1,0:T(8,128)S(1)}, f32[48,128]{1,0:T(8,128)S(1)}, u32[]{:S(2)}, u32[]{:S(2)}) collective-permute-start(f32[48,128]{1,0:T(8,128)S(1)} %get-tuple-element.19), channel_id=1, source_target_pairs={{0,1},{1,2},{2,3},{3,4},{4,5},{5,6},{6,7},{7,8},{8,9},{9,10},{10,1... | collective-permute-start | bytes 73736 | tf_op jit(solution)/shard_map/ppermute | solution.py:347
  29.2 0.0 copy-start
  29.2 0.7 copy-done
  29.9 5.9 %shard_map.79 = (f32[4,18,128,128]{3,2,1,0:T(8,128)S(1)}, f32[4,2,128,128]{3,2,1,0:T(8,128)S(1)}, f32[4,4,128,128]{3,2,1,0:T(8,128)S(1)}, f32[4,9,128]{2,1,0:T(8...) custom-call(f32[16,16,128]{2,1,0:T(8,128)S(1)} %all_to_all.25.received, f32[16,128]{1,0:T(8,128)S(1)} %shard_map.77.own, ...), custom_call_target="tpu_custom_call" | custom-call | tf_op jit(solution)/shard_map/pallas_call | solution.py:38
  35.7 11.6 %collective-permute-start.1 = (f32[48,128]{1,0:T(8,128)S(1)}, f32[48,128]{1,0:T(8,128)S(1)}, u32[]{:S(2)}, u32[]{:S(2)}) collective-permute-start(f32[48,128]{1,0:T(8,128)S(1)} %get-tuple-element.21), channel_id=1, source_target_pairs={{1,0},{2,1},{3,2},{4,3},{5,4},{6,5},{7,6},{8,7},{9,8},{10,9},{11,1... | collective-permute-start | bytes 73736 | tf_op jit(solution)/shard_map/ppermute | solution.py:352
  47.4 0.0 collective-permute-done.below
  47.4 0.9 collective-permute-done.1.above
  48.3 2.7 %shard_map.80 = (f32[4,9,128,128]{3,2,1,0:T(8,128)S(1)}, f32[8,128]{1,0:T(8,128)S(1)}, f32[4,128]{1,0:T(4,128)S(1)}, f32[4,128]{1,0:T(4,128)S(1)}) custom-call(f32[48,128]{1,0:T(8,128)S(1)} %collective-permute-done.below, f32[48,128]{1,0:T(8,128)S(1)} %collective-permute-done.1.above, f32[16,128]{1,0:T(8,128)S(1)} %shard_map.77.own, ...), custom_call_target="tpu_custom_call" | custom-call | tf_op jit(solution)/shard_map/pallas_call | solution.py:38
  51.1 1.9 %collective-permute-start.2 = (f32[4,128]{1,0:T(4,128)S(1)}, f32[4,128]{1,0:T(4,128)S(1)}, u32[]{:S(2)}, u32[]{:S(2)}) collective-permute-start(f32[4,128]{1,0:T(4,128)S(1)} %get-tuple-element.26), channel_id=1, source_target_pairs={{0,1},{1,2},{2,3},{3,4},{4,5},{5,6},{6,7},{7,8},{8,9},{9,10},{10,1... | collective-permute-start | bytes 6152 | tf_op jit(solution)/shard_map/ppermute | solution.py:347
  53.0 7.2 %collective-permute-start.3 = (f32[4,128]{1,0:T(4,128)S(1)}, f32[4,128]{1,0:T(4,128)S(1)}, u32[]{:S(2)}, u32[]{:S(2)}) collective-permute-start(f32[4,128]{1,0:T(4,128)S(1)} %get-tuple-element.28), channel_id=1, source_target_pairs={{1,0},{2,1},{3,2},{4,3},{5,4},{6,5},{7,6},{8,7},{9,8},{10,9},{11,1... | collective-permute-start | bytes 6152 | tf_op jit(solution)/shard_map/ppermute | solution.py:352
  60.2 0.7 collective-permute-done.3
  61.0 13.3 %all_to_all.26.received = f32[16,16,128]{2,1,0:T(8,128)S(1)} all-to-all(f32[16,16,128]{2,1,0:T(8,128)S(1)} %broadcast_in_dim.13), channel_id=1, replica_groups=mesh['gx_0'=2,'gx_1'=2,'gy'=4,'gz_0'=8,'gz_1'=8] {'gx_0','gx_1','gy'}, dimensions={0} | all-to-all | bytes 262144 | tf_op jit(solution)/shard_map/all_to_all | solution.py:357
  74.2 1.5 %shard_map.81 = (f32[8,128]{1,0:T(8,128)S(1)}, f32[4,128]{1,0:T(4,128)S(1)}, f32[4,128]{1,0:T(4,128)S(1)}) custom-call(f32[16,16,128]{2,1,0:T(8,128)S(1)} %all_to_all.26.received, f32[4,18,128,128]{3,2,1,0:T(8,128)S(1)} %get-tuple-element.29.inner, f32[4,9,128,128]{3,2,1,0:T(8,128)S(1)} %get-tuple-element.30.outer, f32[16,128]{1,0:T(8,128)S(1)} %shard_map.77.own, ...), custom_call_target="tpu_custom_call" | custom-call | tf_op jit(solution)/shard_map/pallas_call | solution.py:38
  75.7 1.9 %collective-permute-start.4 = (f32[4,128]{1,0:T(4,128)S(1)}, f32[4,128]{1,0:T(4,128)S(1)}, u32[]{:S(2)}, u32[]{:S(2)}) collective-permute-start(f32[4,128]{1,0:T(4,128)S(1)} %get-tuple-element.31), channel_id=1, source_target_pairs={{0,1},{1,2},{2,3},{3,4},{4,5},{5,6},{6,7},{7,8},{8,9},{9,10},{10,1... | collective-permute-start | bytes 6152 | tf_op jit(solution)/shard_map/ppermute | solution.py:347
  77.6 7.2 %collective-permute-start.5 = (f32[4,128]{1,0:T(4,128)S(1)}, f32[4,128]{1,0:T(4,128)S(1)}, u32[]{:S(2)}, u32[]{:S(2)}) collective-permute-start(f32[4,128]{1,0:T(4,128)S(1)} %get-tuple-element.33), channel_id=1, source_target_pairs={{1,0},{2,1},{3,2},{4,3},{5,4},{6,5},{7,6},{8,7},{9,8},{10,9},{11,1... | collective-permute-start | bytes 6152 | tf_op jit(solution)/shard_map/ppermute | solution.py:352
  84.9 0.0 collective-permute-done.4
  84.9 0.7 collective-permute-done.5
  85.6 12.4 %all_to_all.27.received = f32[16,16,128]{2,1,0:T(8,128)S(1)} all-to-all(f32[16,16,128]{2,1,0:T(8,128)S(1)} %broadcast_in_dim.14), channel_id=1, replica_groups=mesh['gx_0'=2,'gx_1'=2,'gy'=4,'gz_0'=8,'gz_1'=8] {'gx_0','gx_1','gy'}, dimensions={0} | all-to-all | bytes 262144 | tf_op jit(solution)/shard_map/all_to_all | solution.py:357
  98.0 1.6 %shard_map.82 = (f32[8,128]{1,0:T(8,128)S(1)}, f32[1,128]{1,0:T(1,128)S(1)}) custom-call(f32[16,16,128]{2,1,0:T(8,128)S(1)} %all_to_all.27.received, f32[4,18,128,128]{3,2,1,0:T(8,128)S(1)} %get-tuple-element.29.inner, f32[4,9,128,128]{3,2,1,0:T(8,128)S(1)} %get-tuple-element.30.outer, f32[16,128]{1,0:T(8,128)S(1)} %shard_map.77.own, ...), custom_call_target="tpu_custom_call" | custom-call | tf_op jit(solution)/shard_map/pallas_call | solution.py:38
  99.7 10.0 %all_to_all.28 = f32[32,1,128]{2,1,0:T(1,128)S(1)} all-to-all(f32[32,1,128]{2,1,0:T(1,128)S(1)} %broadcast_in_dim.16), channel_id=1, replica_groups=mesh['gx_0'=2,'gx_1'=2,'gy'=4,'gz_0'=8,'gz_1'=8] {'gx_0','gx_1','gz_1'}, dimensions={0} | all-to-all | bytes 32768 | tf_op jit(solution)/shard_map/all_to_all | solution.py:357
  109.7 18.8 %all_to_all.29.received = f32[32,1,128]{2,1,0:T(1,128)S(1)} all-to-all(f32[32,1,128]{2,1,0:T(1,128)S(1)} %broadcast_in_dim.17), channel_id=1, replica_groups=mesh['gx_0'=2,'gx_1'=2,'gy'=4,'gz_0'=8,'gz_1'=8] {'gy','gz_0'}, dimensions={0} | all-to-all | bytes 32768 | tf_op jit(solution)/shard_map/all_to_all | solution.py:357
  128.5 0.7 shard_map.83
  (10 shorter events, 0.1 us)
Async XLA Ops:
  27.2 20.2 %collective-permute-start = (f32[48,128]{1,0:T(8,128)S(1)}, f32[48,128]{1,0:T(8,128)S(1)}, u32[]{:S(2)}, u32[]{:S(2)}) collective-permute-start(f32[48,128]{1,0:T(8,128)S(1)} %get-tuple-element.19), channel_id=1, source_target_pairs={{0,1},{1,2},{2,3},{3,4},{4,5},{5,6},{6,7},{7,8},{8,9},{9,10},{10,1... | collective-permute-start | bytes 73736 | tf_op jit(solution)/shard_map/ppermute | solution.py:347
  29.2 0.7 copy-start
  35.7 12.6 %collective-permute-start.1 = (f32[48,128]{1,0:T(8,128)S(1)}, f32[48,128]{1,0:T(8,128)S(1)}, u32[]{:S(2)}, u32[]{:S(2)}) collective-permute-start(f32[48,128]{1,0:T(8,128)S(1)} %get-tuple-element.21), channel_id=1, source_target_pairs={{1,0},{2,1},{3,2},{4,3},{5,4},{6,5},{7,6},{8,7},{9,8},{10,9},{11,1... | collective-permute-start | bytes 73736 | tf_op jit(solution)/shard_map/ppermute | solution.py:352
  51.1 9.2 %collective-permute-start.2 = (f32[4,128]{1,0:T(4,128)S(1)}, f32[4,128]{1,0:T(4,128)S(1)}, u32[]{:S(2)}, u32[]{:S(2)}) collective-permute-start(f32[4,128]{1,0:T(4,128)S(1)} %get-tuple-element.26), channel_id=1, source_target_pairs={{0,1},{1,2},{2,3},{3,4},{4,5},{5,6},{6,7},{7,8},{8,9},{9,10},{10,1... | collective-permute-start | bytes 6152 | tf_op jit(solution)/shard_map/ppermute | solution.py:347
  53.0 8.0 %collective-permute-start.3 = (f32[4,128]{1,0:T(4,128)S(1)}, f32[4,128]{1,0:T(4,128)S(1)}, u32[]{:S(2)}, u32[]{:S(2)}) collective-permute-start(f32[4,128]{1,0:T(4,128)S(1)} %get-tuple-element.28), channel_id=1, source_target_pairs={{1,0},{2,1},{3,2},{4,3},{5,4},{6,5},{7,6},{8,7},{9,8},{10,9},{11,1... | collective-permute-start | bytes 6152 | tf_op jit(solution)/shard_map/ppermute | solution.py:352
  75.7 9.2 %collective-permute-start.4 = (f32[4,128]{1,0:T(4,128)S(1)}, f32[4,128]{1,0:T(4,128)S(1)}, u32[]{:S(2)}, u32[]{:S(2)}) collective-permute-start(f32[4,128]{1,0:T(4,128)S(1)} %get-tuple-element.31), channel_id=1, source_target_pairs={{0,1},{1,2},{2,3},{3,4},{4,5},{5,6},{6,7},{7,8},{8,9},{9,10},{10,1... | collective-permute-start | bytes 6152 | tf_op jit(solution)/shard_map/ppermute | solution.py:347
  77.6 7.9 %collective-permute-start.5 = (f32[4,128]{1,0:T(4,128)S(1)}, f32[4,128]{1,0:T(4,128)S(1)}, u32[]{:S(2)}, u32[]{:S(2)}) collective-permute-start(f32[4,128]{1,0:T(4,128)S(1)} %get-tuple-element.33), channel_id=1, source_target_pairs={{1,0},{2,1},{3,2},{4,3},{5,4},{6,5},{7,6},{8,7},{9,8},{10,9},{11,1... | collective-permute-start | bytes 6152 | tf_op jit(solution)/shard_map/ppermute | solution.py:352

commit v3 on v2

--- a/solution.py
+++ b/solution.py
@@ -11,8 +11,8 @@
 GX = ("gx_0", "gx_1")
 GZ = ("gz_0", "gz_1")
 PLANE = ("gx_0", "gx_1", "gy")
-GROUP_ONE = ("gx_0", "gx_1", "gz_1")
-GROUP_TWO = ("gy", "gz_0")
+GROUP_ONE = ("gx_0", "gx_1", "gy", "gz_1")
+GROUP_TWO = ("gz_0",)
 
 CELL_EDGE = 11.0
 CUTOFF = 10.0
@@ -138,15 +138,14 @@
 
 
 def inner_body(
-    received, own, neighbours, chi, eta, gamma, face,
-    blocks, acc, columns, away_outer, table, face_out, near, away,
+    received, own, neighbours, chi, eta, gamma,
+    blocks, acc, columns, away_outer, table, near, away,
 ):
     for kind in range(2):
         value = jnp.full((1, ATOMS), gamma[kind], F32)
         table[kind : kind + 1, :] = 1.0 / (value * jnp.sqrt(value))
         table[2 + kind : 3 + kind, :] = jnp.full((1, ATOMS), chi[kind], F32)
         table[4 + kind : 5 + kind, :] = jnp.full((1, ATOMS), eta[kind], F32)
-    face_out[...] = face[...]
     for b in range(2):
         for c in range(2):
             tile = b * 2 + c
@@ -379,17 +378,16 @@
     )
     received = shared(own, PLANE)
     head, tail = run(faces_body, [(48, ATOMS), (48, ATOMS)], (received,))
-    below = upward(tail)
+    below, above = upward(tail), downward(head)
     products = (4, 2, ATOMS, ATOMS)
     accumulate = VMEM(products, F32)
-    inner, partial, columns, away, table, head = run(
+    inner, partial, columns, away, table = run(
         inner_body,
-        [(4, 18, ATOMS, ATOMS), products, (4, FIELDS, ATOMS, ATOMS), (4, 9, ATOMS), (8, ATOMS), (48, ATOMS)],
-        (received, own, neighbours, type_chi, type_eta, type_gamma, head),
-        [VMEM, VMEM, VMEM, smem, smem, smem, VMEM],
+        [(4, 18, ATOMS, ATOMS), products, (4, FIELDS, ATOMS, ATOMS), (4, 9, ATOMS), (8, ATOMS)],
+        (received, own, neighbours, type_chi, type_eta, type_gamma),
+        [VMEM, VMEM, VMEM, smem, smem, smem],
         [VMEM((5, 24, 8, ATOMS), F32), VMEM((4, 18, ATOMS), F32)],
     )
-    above = downward(head)
     vectors = [(8, ATOMS), (4, ATOMS), (4, ATOMS)]
     outer, w1, head, tail = run(
         outer_body,

time: 130 us -> 127 us (0.977)
  transfers between devices with their start and end apart: 6 -> 6, of which waited for: 3 -> 2; matrix products, arithmetic and copies ran while one was open for 0% -> 0% of each run, Pallas kernels for 5% -> 5%
where the time goes in v3:
time: 127 us
  blocking collectives  79.4 us (63%)
  starting transfers between devices  31.3 us (25%)
  Pallas kernels  13.2 us (10%)
  waiting for transfers between devices  1.42 us (1%)
    all_to_all x5, blocking collectives, shared(): lax.all_to_all(jnp.broadcast_to(block[None], (count,) + block.shape), axe...  79.4 us
    ppermute x3, starting transfers between devices, downward(): return lax.ppermute(head, GZ, [((i + 1) % count, i) for i in range(count)])  25.5 us
    pallas_call x6, Pallas kernels, run(): pl.pallas_call(body, out_shape=tuple((VMEM(shape, F32) for shape in outs)...  12.4 us
    ppermute x3, starting transfers between devices, upward(): return lax.ppermute(tail, GZ, [(i, (i + 1) % count) for i in range(count)])  5.76 us
  transfers between devices with their start and end apart: 6, of which 2 were waited for; matrix products, arithmetic and copies ran while one was open for 0% of the time, Pallas kernels for 5%

profile of v3, /device:TPU:1, one launch (start us, length us, event | category | flops | bytes accessed | tf_op | source)
XLA Modules:
  0.0 126.9 jit_solution(5962623036680805514)
XLA Ops:
  0.6 0.7 shard_map.77.own
  1.4 25.8 %all_to_all.25.received = f32[16,16,128]{2,1,0:T(8,128)S(1)} all-to-all(f32[16,16,128]{2,1,0:T(8,128)S(1)} %broadcast_in_dim.12), channel_id=1, replica_groups=mesh['gx_0'=2,'gx_1'=2,'gy'=4,'gz_0'=8,'gz_1'=8] {'gx_0','gx_1','gy'}, dimensions={0} | all-to-all | bytes 262144 | tf_op jit(solution)/shard_map/all_to_all | solution.py:356
  27.2 1.9 %collective-permute-start = (f32[48,128]{1,0:T(8,128)S(1)}, f32[48,128]{1,0:T(8,128)S(1)}, u32[]{:S(2)}, u32[]{:S(2)}) collective-permute-start(f32[48,128]{1,0:T(8,128)S(1)} %get-tuple-element.18), channel_id=1, source_target_pairs={{0,1},{1,2},{2,3},{3,4},{4,5},{5,6},{6,7},{7,8},{8,9},{9,10},{10,1... | collective-permute-start | bytes 73736 | tf_op jit(solution)/shard_map/ppermute | solution.py:346
  29.2 11.6 %collective-permute-start.1 = (f32[48,128]{1,0:T(8,128)S(1)}, f32[48,128]{1,0:T(8,128)S(1)}, u32[]{:S(2)}, u32[]{:S(2)}) collective-permute-start(f32[48,128]{1,0:T(8,128)S(1)} %get-tuple-element.19), channel_id=1, source_target_pairs={{1,0},{2,1},{3,2},{4,3},{5,4},{6,5},{7,6},{8,7},{9,8},{10,9},{11,1... | collective-permute-start | bytes 73736 | tf_op jit(solution)/shard_map/ppermute | solution.py:351
  40.8 0.0 copy-start
  40.8 0.7 copy-done
  41.5 5.9 %shard_map.79 = (f32[4,18,128,128]{3,2,1,0:T(8,128)S(1)}, f32[4,2,128,128]{3,2,1,0:T(8,128)S(1)}, f32[4,4,128,128]{3,2,1,0:T(8,128)S(1)}, f32[4,9,128]{2,1,0:T(8,128)S(1)}, f32[8,128]{1,0:T(8,128)S(1)}) custom-call(f32[16,16,128]{2,1,0:T(8,128)S(1)} %all_to_all.25.received, f32[16,128]{1,0:T(8,128)S(1)} %shard_map.77.own, s32[1,2,2,27]{3,2,1,0:T(2,128)S(1)} %copy-done, ...), custom_call_target="tpu_custom_call" | custom-call | tf_op jit(solution)/shard_map/pallas_call | solution.py:38
  47.4 0.0 collective-permute-done.below
  47.4 0.0 collective-permute-done.1.above
  47.4 2.7 %shard_map.80 = (f32[4,9,128,128]{3,2,1,0:T(8,128)S(1)}, f32[8,128]{1,0:T(8,128)S(1)}, f32[4,128]{1,0:T(4,128)S(1)}, f32[4,128]{1,0:T(4,128)S(1)}) custom-call(f32[48,128]{1,0:T(8,128)S(1)} %collective-permute-done.below, f32[48,128]{1,0:T(8,128)S(1)} %collective-permute-done.1.above, f32[16,128]{1,0:T(8,128)S(1)} %shard_map.77.own, ...), custom_call_target="tpu_custom_call" | custom-call | tf_op jit(solution)/shard_map/pallas_call | solution.py:38
  50.1 1.9 %collective-permute-start.2 = (f32[4,128]{1,0:T(4,128)S(1)}, f32[4,128]{1,0:T(4,128)S(1)}, u32[]{:S(2)}, u32[]{:S(2)}) collective-permute-start(f32[4,128]{1,0:T(4,128)S(1)} %get-tuple-element.24), channel_id=1, source_target_pairs={{0,1},{1,2},{2,3},{3,4},{4,5},{5,6},{6,7},{7,8},{8,9},{9,10},{10,1... | collective-permute-start | bytes 6152 | tf_op jit(solution)/shard_map/ppermute | solution.py:346
  52.1 6.7 %collective-permute-start.3 = (f32[4,128]{1,0:T(4,128)S(1)}, f32[4,128]{1,0:T(4,128)S(1)}, u32[]{:S(2)}, u32[]{:S(2)}) collective-permute-start(f32[4,128]{1,0:T(4,128)S(1)} %get-tuple-element.26), channel_id=1, source_target_pairs={{1,0},{2,1},{3,2},{4,3},{5,4},{6,5},{7,6},{8,7},{9,8},{10,9},{11,1... | collective-permute-start | bytes 6152 | tf_op jit(solution)/shard_map/ppermute | solution.py:351
  58.8 0.7 collective-permute-done.3
  59.5 13.0 %all_to_all.26.received = f32[16,16,128]{2,1,0:T(8,128)S(1)} all-to-all(f32[16,16,128]{2,1,0:T(8,128)S(1)} %broadcast_in_dim.13), channel_id=1, replica_groups=mesh['gx_0'=2,'gx_1'=2,'gy'=4,'gz_0'=8,'gz_1'=8] {'gx_0','gx_1','gy'}, dimensions={0} | all-to-all | bytes 262144 | tf_op jit(solution)/shard_map/all_to_all | solution.py:356
  72.5 1.5 %shard_map.81 = (f32[8,128]{1,0:T(8,128)S(1)}, f32[4,128]{1,0:T(4,128)S(1)}, f32[4,128]{1,0:T(4,128)S(1)}) custom-call(f32[16,16,128]{2,1,0:T(8,128)S(1)} %all_to_all.26.received, f32[4,18,128,128]{3,2,1,0:T(8,128)S(1)} %get-tuple-element.27.inner, f32[4,9,128,128]{3,2,1,0:T(8,128)S(1)} %get-tuple-element.28.outer, f32[16,128]{1,0:T(8,128)S(1)} %shard_map.77.own, ...), custom_call_target="tpu_custom_call" | custom-call | tf_op jit(solution)/shard_map/pallas_call | solution.py:38
  74.0 1.9 %collective-permute-start.4 = (f32[4,128]{1,0:T(4,128)S(1)}, f32[4,128]{1,0:T(4,128)S(1)}, u32[]{:S(2)}, u32[]{:S(2)}) collective-permute-start(f32[4,128]{1,0:T(4,128)S(1)} %get-tuple-element.29), channel_id=1, source_target_pairs={{0,1},{1,2},{2,3},{3,4},{4,5},{5,6},{6,7},{7,8},{8,9},{9,10},{10,1... | collective-permute-start | bytes 6152 | tf_op jit(solution)/shard_map/ppermute | solution.py:346
  75.9 7.2 %collective-permute-start.5 = (f32[4,128]{1,0:T(4,128)S(1)}, f32[4,128]{1,0:T(4,128)S(1)}, u32[]{:S(2)}, u32[]{:S(2)}) collective-permute-start(f32[4,128]{1,0:T(4,128)S(1)} %get-tuple-element.31), channel_id=1, source_target_pairs={{1,0},{2,1},{3,2},{4,3},{5,4},{6,5},{7,6},{8,7},{9,8},{10,9},{11,1... | collective-permute-start | bytes 6152 | tf_op jit(solution)/shard_map/ppermute | solution.py:351
  83.1 0.0 collective-permute-done.4
  83.1 0.7 collective-permute-done.5
  83.9 12.4 %all_to_all.27.received = f32[16,16,128]{2,1,0:T(8,128)S(1)} all-to-all(f32[16,16,128]{2,1,0:T(8,128)S(1)} %broadcast_in_dim.14), channel_id=1, replica_groups=mesh['gx_0'=2,'gx_1'=2,'gy'=4,'gz_0'=8,'gz_1'=8] {'gx_0','gx_1','gy'}, dimensions={0} | all-to-all | bytes 262144 | tf_op jit(solution)/shard_map/all_to_all | solution.py:356
  96.3 1.6 %shard_map.82 = (f32[8,128]{1,0:T(8,128)S(1)}, f32[1,128]{1,0:T(1,128)S(1)}) custom-call(f32[16,16,128]{2,1,0:T(8,128)S(1)} %all_to_all.27.received, f32[4,18,128,128]{3,2,1,0:T(8,128)S(1)} %get-tuple-element.27.inner, f32[4,9,128,128]{3,2,1,0:T(8,128)S(1)} %get-tuple-element.28.outer, f32[16,128]{1,0:T(8,128)S(1)} %shard_map.77.own, ...), custom_call_target="tpu_custom_call" | custom-call | tf_op jit(solution)/shard_map/pallas_call | solution.py:38
  97.9 15.7 %all_to_all.28 = f32[128,1,128]{2,1,0:T(1,128)S(1)} all-to-all(f32[128,1,128]{2,1,0:T(1,128)S(1)} %broadcast_in_dim.16), channel_id=1, replica_groups=mesh['gx_0'=2,'gx_1'=2,'gy'=4,'gz_0'=8,'gz_1'=8] {'gx_0','gx_1','gy','gz..., dimensions={0} | all-to-all | bytes 131072 | tf_op jit(solution)/shard_map/all_to_all | solution.py:356
  113.6 12.5 %all_to_all.29.received = f32[8,1,128]{2,1,0:T(1,128)S(1)} all-to-all(f32[8,1,128]{2,1,0:T(1,128)S(1)} %broadcast_in_dim.17), channel_id=1, replica_groups=mesh['gx_0'=2,'gx_1'=2,'gy'=4,'gz_0'=8,'gz_1'=8] {'gz_0'}, dimensions={0} | all-to-all | bytes 8192 | tf_op jit(solution)/shard_map/all_to_all | solution.py:356
  126.2 0.7 shard_map.83
  (10 shorter events, 0.2 us)
Async XLA Ops:
  27.2 20.2 %collective-permute-start = (f32[48,128]{1,0:T(8,128)S(1)}, f32[48,128]{1,0:T(8,128)S(1)}, u32[]{:S(2)}, u32[]{:S(2)}) collective-permute-start(f32[48,128]{1,0:T(8,128)S(1)} %get-tuple-element.18), channel_id=1, source_target_pairs={{0,1},{1,2},{2,3},{3,4},{4,5},{5,6},{6,7},{7,8},{8,9},{9,10},{10,1... | collective-permute-start | bytes 73736 | tf_op jit(solution)/shard_map/ppermute | solution.py:346
  29.2 18.2 %collective-permute-start.1 = (f32[48,128]{1,0:T(8,128)S(1)}, f32[48,128]{1,0:T(8,128)S(1)}, u32[]{:S(2)}, u32[]{:S(2)}) collective-permute-start(f32[48,128]{1,0:T(8,128)S(1)} %get-tuple-element.19), channel_id=1, source_target_pairs={{1,0},{2,1},{3,2},{4,3},{5,4},{6,5},{7,6},{8,7},{9,8},{10,9},{11,1... | collective-permute-start | bytes 73736 | tf_op jit(solution)/shard_map/ppermute | solution.py:351
  40.8 0.7 copy-start
  50.1 8.6 %collective-permute-start.2 = (f32[4,128]{1,0:T(4,128)S(1)}, f32[4,128]{1,0:T(4,128)S(1)}, u32[]{:S(2)}, u32[]{:S(2)}) collective-permute-start(f32[4,128]{1,0:T(4,128)S(1)} %get-tuple-element.24), channel_id=1, source_target_pairs={{0,1},{1,2},{2,3},{3,4},{4,5},{5,6},{6,7},{7,8},{8,9},{9,10},{10,1... | collective-permute-start | bytes 6152 | tf_op jit(solution)/shard_map/ppermute | solution.py:346
  52.1 7.4 %collective-permute-start.3 = (f32[4,128]{1,0:T(4,128)S(1)}, f32[4,128]{1,0:T(4,128)S(1)}, u32[]{:S(2)}, u32[]{:S(2)}) collective-permute-start(f32[4,128]{1,0:T(4,128)S(1)} %get-tuple-element.26), channel_id=1, source_target_pairs={{1,0},{2,1},{3,2},{4,3},{5,4},{6,5},{7,6},{8,7},{9,8},{10,9},{11,1... | collective-permute-start | bytes 6152 | tf_op jit(solution)/shard_map/ppermute | solution.py:351
  74.0 9.2 %collective-permute-start.4 = (f32[4,128]{1,0:T(4,128)S(1)}, f32[4,128]{1,0:T(4,128)S(1)}, u32[]{:S(2)}, u32[]{:S(2)}) collective-permute-start(f32[4,128]{1,0:T(4,128)S(1)} %get-tuple-element.29), channel_id=1, source_target_pairs={{0,1},{1,2},{2,3},{3,4},{4,5},{5,6},{6,7},{7,8},{8,9},{9,10},{10,1... | collective-permute-start | bytes 6152 | tf_op jit(solution)/shard_map/ppermute | solution.py:346
  75.9 7.9 %collective-permute-start.5 = (f32[4,128]{1,0:T(4,128)S(1)}, f32[4,128]{1,0:T(4,128)S(1)}, u32[]{:S(2)}, u32[]{:S(2)}) collective-permute-start(f32[4,128]{1,0:T(4,128)S(1)} %get-tuple-element.31), channel_id=1, source_target_pairs={{1,0},{2,1},{3,2},{4,3},{5,4},{6,5},{7,6},{8,7},{9,8},{10,9},{11,1... | collective-permute-start | bytes 6152 | tf_op jit(solution)/shard_map/ppermute | solution.py:351

commit v4 on v3

--- a/solution.py
+++ b/solution.py
@@ -11,15 +11,15 @@
 GX = ("gx_0", "gx_1")
 GZ = ("gz_0", "gz_1")
 PLANE = ("gx_0", "gx_1", "gy")
-GROUP_ONE = ("gx_0", "gx_1", "gy", "gz_1")
-GROUP_TWO = ("gz_0",)
+GROUP_ONE = ("gx_0", "gx_1", "gz_1")
+GROUP_TWO = ("gy", "gz_0")
 
 CELL_EDGE = 11.0
 CUTOFF = 10.0
 SCALE = 14.4 * 0.02 / CUTOFF**4
 FAR = 1.0e4
 ATOMS = 128
-GROUPS = 8
+GROUPS = ATOMS // 8
 FIELDS = 4
 SHIFTS = (200.0, 100.0, 20.0)
 INNER = tuple((ix, jy, k) for ix in range(3) for jy in range(3) for k in range(2))
@@ -29,11 +29,11 @@
 F32 = jnp.float32
 
 
-def run(body, outs, args, spaces=None, scratch=()):
+def run(body, outs, args, spaces=None, scratch=(), far=()):
     spaces = spaces or [VMEM] * len(args)
     held = [
-        pltpu.with_memory_space_constraint(x, VMEM if space == VMEM else HBM)
-        for x, space in zip(args, spaces)
+        pltpu.with_memory_space_constraint(x, VMEM if space == VMEM and n not in far else HBM)
+        for n, (x, space) in enumerate(zip(args, spaces))
     ]
     return pl.pallas_call(
         body,
@@ -98,11 +98,11 @@
     return jnp.sum(acc.T, axis=0, keepdims=True)
 
 
-def couple(near, columns, away, tile, start, p, line, blocks, slot, sums_s, sums_t, mask):
+def couple(near, columns, away, tile, p, line, blocks, slot, sums_s, sums_t, mask):
     xj = near[0, p] + away[tile, line : line + 1, :]
     yj, zj, sj, cj = near[1, p], near[2, p], near[3, p], near[4, p]
     for g in range(GROUPS):
-        rows = pl.ds(pl.multiple_of(start + g * 8, 8), 8)
+        rows = pl.ds(g * 8, 8)
         dx = xj - columns[tile, 0, rows, :]
         dy = yj - columns[tile, 1, rows, :]
         dz = zj - columns[tile, 2, rows, :]
@@ -120,9 +120,9 @@
         sums_s[g] = sums_s[g] + value * cj
 
 
-def store(acc, tile, start, sums_s, sums_t):
+def store(acc, tile, sums_s, sums_t):
     for g in range(GROUPS):
-        rows = pl.ds(pl.multiple_of(start + g * 8, 8), 8)
+        rows = pl.ds(g * 8, 8)
         acc[tile, 0, rows, :] = sums_s[g]
         acc[tile, 1, rows, :] = sums_t[g]
 
@@ -174,23 +174,21 @@
     lane = lax.broadcasted_iota(jnp.int32, (8, ATOMS), 1)
     sub = lax.broadcasted_iota(jnp.int32, (8, ATOMS), 0)
 
-    def half_tile(step, carry):
-        tile = step // 2
+    def one_tile(tile, carry):
         b, c = tile // 2, tile % 2
-        start = (step % 2) * (GROUPS * 8)
         sums_s = [jnp.zeros((8, ATOMS), F32) for _ in range(GROUPS)]
         sums_t = [jnp.zeros((8, ATOMS), F32) for _ in range(GROUPS)]
         for slot, (ix, jy, k) in enumerate(INNER):
             mask = None
             if (ix, jy) == (1, 1):
-                first = start + jnp.where(c == k, 0, 2 * ATOMS)
+                first = jnp.where(c == k, 0, 2 * ATOMS)
                 mask = functools.partial(lambda at, g: lane == sub + (at + g * 8), first)
             p = (ix * 4 + jy + b) * 2 + k
-            couple(near, columns, away, tile, start, p, slot, blocks, slot, sums_s, sums_t, mask)
-        store(acc, tile, start, sums_s, sums_t)
+            couple(near, columns, away, tile, p, slot, blocks, slot, sums_s, sums_t, mask)
+        store(acc, tile, sums_s, sums_t)
         return carry
 
-    lax.fori_loop(0, 8, half_tile, 0)
+    lax.fori_loop(0, 4, one_tile, 0)
 
 
 def outer_body(
@@ -204,20 +202,18 @@
                 lines = [ghost[line + f : line + f + 1, :] for f in range(FIELDS)]
                 place(near, (ix * 4 + iy) * 2 + side, lines, table, lift)
 
-    def half_tile(step, carry):
-        tile = step // 2
+    def one_tile(tile, carry):
         b, c = tile // 2, tile % 2
-        start = (step % 2) * (GROUPS * 8)
-        rows = [pl.ds(pl.multiple_of(start + g * 8, 8), 8) for g in range(GROUPS)]
+        rows = [pl.ds(g * 8, 8) for g in range(GROUPS)]
         sums_s = [partial[tile, 0, r, :] for r in rows]
         sums_t = [partial[tile, 1, r, :] for r in rows]
         for slot, (ix, jy) in enumerate(OUTER):
             p = (ix * 4 + jy + b) * 2 + c
-            couple(near, columns, away, tile, start, p, slot, blocks, slot, sums_s, sums_t, None)
-        store(acc, tile, start, sums_s, sums_t)
+            couple(near, columns, away, tile, p, slot, blocks, slot, sums_s, sums_t, None)
+        store(acc, tile, sums_s, sums_t)
         return carry
 
-    lax.fori_loop(0, 8, half_tile, 0)
+    lax.fori_loop(0, 4, one_tile, 0)
     source = source_rows(own, table)
     next_vector(own, table, source, acc, out, SHIFTS[0], (-SCALE, -SCALE))
     head[...] = out[0:4, :]
@@ -387,6 +383,7 @@
         (received, own, neighbours, type_chi, type_eta, type_gamma),
         [VMEM, VMEM, VMEM, smem, smem, smem],
         [VMEM((5, 24, 8, ATOMS), F32), VMEM((4, 18, ATOMS), F32)],
+        far=(2,),
     )
     vectors = [(8, ATOMS), (4, ATOMS), (4, ATOMS)]
     outer, w1, head, tail = run(

time: 127 us -> 127 us (level)
  no operation moved by 1% of the time
where the time goes in v4:
time: 127 us
  blocking collectives  80 us (63%)
  starting transfers between devices  31.3 us (25%)
  Pallas kernels  13.2 us (10%)
  waiting for transfers between devices  1.42 us (1%)
    all_to_all x5, blocking collectives, shared(): lax.all_to_all(jnp.broadcast_to(block[None], (count,) + block.shape), axe...  80 us
    ppermute x3, starting transfers between devices, downward(): return lax.ppermute(head, GZ, [((i + 1) % count, i) for i in range(count)])  25.5 us
    pallas_call x6, Pallas kernels, run(): pl.pallas_call(body, out_shape=tuple((VMEM(shape, F32) for shape in outs)...  12.4 us
    ppermute x3, starting transfers between devices, upward(): return lax.ppermute(tail, GZ, [(i, (i + 1) % count) for i in range(count)])  5.76 us
  transfers between devices with their start and end apart: 6, of which 2 were waited for; matrix products, arithmetic and copies ran while one was open for 0% of the time, Pallas kernels for 5%

profile of v4, /device:TPU:1, one launch (start us, length us, event | category | flops | bytes accessed | tf_op | source)
XLA Modules:
  0.0 126.8 jit_solution(379689078673143087)
XLA Ops:
  0.6 0.7 shard_map.77.own
  1.4 25.8 %all_to_all.25.received = f32[16,16,128]{2,1,0:T(8,128)S(1)} all-to-all(f32[16,16,128]{2,1,0:T(8,128)S(1)} %broadcast_in_dim.12), channel_id=1, replica_groups=mesh['gx_0'=2,'gx_1'=2,'gy'=4,'gz_0'=8,'gz_1'=8] {'gx_0','gx_1','gy'}, dimensions={0} | all-to-all | bytes 262144 | tf_op jit(solution)/shard_map/all_to_all | solution.py:352
  27.2 1.9 %collective-permute-start = (f32[48,128]{1,0:T(8,128)S(1)}, f32[48,128]{1,0:T(8,128)S(1)}, u32[]{:S(2)}, u32[]{:S(2)}) collective-permute-start(f32[48,128]{1,0:T(8,128)S(1)} %get-tuple-element.18), channel_id=1, source_target_pairs={{0,1},{1,2},{2,3},{3,4},{4,5},{5,6},{6,7},{7,8},{8,9},{9,10},{10,1... | collective-permute-start | bytes 73736 | tf_op jit(solution)/shard_map/ppermute | solution.py:342
  29.2 11.6 %collective-permute-start.1 = (f32[48,128]{1,0:T(8,128)S(1)}, f32[48,128]{1,0:T(8,128)S(1)}, u32[]{:S(2)}, u32[]{:S(2)}) collective-permute-start(f32[48,128]{1,0:T(8,128)S(1)} %get-tuple-element.19), channel_id=1, source_target_pairs={{1,0},{2,1},{3,2},{4,3},{5,4},{6,5},{7,6},{8,7},{9,8},{10,9},{11,1... | collective-permute-start | bytes 73736 | tf_op jit(solution)/shard_map/ppermute | solution.py:347
  40.8 6.0 %shard_map.79 = (f32[4,18,128,128]{3,2,1,0:T(8,128)S(1)}, f32[4,2,128,128]{3,2,1,0:T(8,128)S(1)}, f32[4,4,128,128]{3,2,1,0:T(8,128)S(1)}, f32[4,9,128]{2,1,0:T(8,128)S(1)}, f32[8,128]{1,0:T(8,128)S(1)}) custom-call(f32[16,16,128]{2,1,0:T(8,128)S(1)} %all_to_all.25.received, f32[16,128]{1,0:T(8,128)S(1)} %shard_map.77.own, s32[1,2,2,27]{3,2,1,0:T(2,128)} %neighbours.1, ...), custom_call_target="tpu_custom_call" | custom-call | tf_op jit(solution)/shard_map/pallas_call | solution.py:38
  46.8 0.0 collective-permute-done.below
  46.8 0.0 collective-permute-done.1.above
  46.8 2.6 %shard_map.80 = (f32[4,9,128,128]{3,2,1,0:T(8,128)S(1)}, f32[8,128]{1,0:T(8,128)S(1)}, f32[4,128]{1,0:T(4,128)S(1)}, f32[4,128]{1,0:T(4,128)S(1)}) custom-call(f32[48,128]{1,0:T(8,128)S(1)} %collective-permute-done.below, f32[48,128]{1,0:T(8,128)S(1)} %collective-permute-done.1.above, f32[16,128]{1,0:T(8,128)S(1)} %shard_map.77.own, ...), custom_call_target="tpu_custom_call" | custom-call | tf_op jit(solution)/shard_map/pallas_call | solution.py:38
  49.4 1.9 %collective-permute-start.2 = (f32[4,128]{1,0:T(4,128)S(1)}, f32[4,128]{1,0:T(4,128)S(1)}, u32[]{:S(2)}, u32[]{:S(2)}) collective-permute-start(f32[4,128]{1,0:T(4,128)S(1)} %get-tuple-element.24), channel_id=1, source_target_pairs={{0,1},{1,2},{2,3},{3,4},{4,5},{5,6},{6,7},{7,8},{8,9},{9,10},{10,1... | collective-permute-start | bytes 6152 | tf_op jit(solution)/shard_map/ppermute | solution.py:342
  51.4 6.7 %collective-permute-start.3 = (f32[4,128]{1,0:T(4,128)S(1)}, f32[4,128]{1,0:T(4,128)S(1)}, u32[]{:S(2)}, u32[]{:S(2)}) collective-permute-start(f32[4,128]{1,0:T(4,128)S(1)} %get-tuple-element.26), channel_id=1, source_target_pairs={{1,0},{2,1},{3,2},{4,3},{5,4},{6,5},{7,6},{8,7},{9,8},{10,9},{11,1... | collective-permute-start | bytes 6152 | tf_op jit(solution)/shard_map/ppermute | solution.py:347
  58.1 0.0 collective-permute-done.2
  58.1 0.7 collective-permute-done.3
  58.8 13.0 %all_to_all.26.received = f32[16,16,128]{2,1,0:T(8,128)S(1)} all-to-all(f32[16,16,128]{2,1,0:T(8,128)S(1)} %broadcast_in_dim.13), channel_id=1, replica_groups=mesh['gx_0'=2,'gx_1'=2,'gy'=4,'gz_0'=8,'gz_1'=8] {'gx_0','gx_1','gy'}, dimensions={0} | all-to-all | bytes 262144 | tf_op jit(solution)/shard_map/all_to_all | solution.py:352
  71.8 1.5 %shard_map.81 = (f32[8,128]{1,0:T(8,128)S(1)}, f32[4,128]{1,0:T(4,128)S(1)}, f32[4,128]{1,0:T(4,128)S(1)}) custom-call(f32[16,16,128]{2,1,0:T(8,128)S(1)} %all_to_all.26.received, f32[4,18,128,128]{3,2,1,0:T(8,128)S(1)} %get-tuple-element.27.inner, f32[4,9,128,128]{3,2,1,0:T(8,128)S(1)} %get-tuple-element.28.outer, f32[16,128]{1,0:T(8,128)S(1)} %shard_map.77.own, ...), custom_call_target="tpu_custom_call" | custom-call | tf_op jit(solution)/shard_map/pallas_call | solution.py:38
  73.3 1.9 %collective-permute-start.4 = (f32[4,128]{1,0:T(4,128)S(1)}, f32[4,128]{1,0:T(4,128)S(1)}, u32[]{:S(2)}, u32[]{:S(2)}) collective-permute-start(f32[4,128]{1,0:T(4,128)S(1)} %get-tuple-element.29), channel_id=1, source_target_pairs={{0,1},{1,2},{2,3},{3,4},{4,5},{5,6},{6,7},{7,8},{8,9},{9,10},{10,1... | collective-permute-start | bytes 6152 | tf_op jit(solution)/shard_map/ppermute | solution.py:342
  75.2 7.2 %collective-permute-start.5 = (f32[4,128]{1,0:T(4,128)S(1)}, f32[4,128]{1,0:T(4,128)S(1)}, u32[]{:S(2)}, u32[]{:S(2)}) collective-permute-start(f32[4,128]{1,0:T(4,128)S(1)} %get-tuple-element.31), channel_id=1, source_target_pairs={{1,0},{2,1},{3,2},{4,3},{5,4},{6,5},{7,6},{8,7},{9,8},{10,9},{11,1... | collective-permute-start | bytes 6152 | tf_op jit(solution)/shard_map/ppermute | solution.py:347
  82.4 0.0 collective-permute-done.4
  82.4 0.7 collective-permute-done.5
  83.2 12.4 %all_to_all.27.received = f32[16,16,128]{2,1,0:T(8,128)S(1)} all-to-all(f32[16,16,128]{2,1,0:T(8,128)S(1)} %broadcast_in_dim.14), channel_id=1, replica_groups=mesh['gx_0'=2,'gx_1'=2,'gy'=4,'gz_0'=8,'gz_1'=8] {'gx_0','gx_1','gy'}, dimensions={0} | all-to-all | bytes 262144 | tf_op jit(solution)/shard_map/all_to_all | solution.py:352
  95.6 1.6 %shard_map.82 = (f32[8,128]{1,0:T(8,128)S(1)}, f32[1,128]{1,0:T(1,128)S(1)}) custom-call(f32[16,16,128]{2,1,0:T(8,128)S(1)} %all_to_all.27.received, f32[4,18,128,128]{3,2,1,0:T(8,128)S(1)} %get-tuple-element.27.inner, f32[4,9,128,128]{3,2,1,0:T(8,128)S(1)} %get-tuple-element.28.outer, f32[16,128]{1,0:T(8,128)S(1)} %shard_map.77.own, ...), custom_call_target="tpu_custom_call" | custom-call | tf_op jit(solution)/shard_map/pallas_call | solution.py:38
  97.2 10.0 %all_to_all.28 = f32[32,1,128]{2,1,0:T(1,128)S(1)} all-to-all(f32[32,1,128]{2,1,0:T(1,128)S(1)} %broadcast_in_dim.16), channel_id=1, replica_groups=mesh['gx_0'=2,'gx_1'=2,'gy'=4,'gz_0'=8,'gz_1'=8] {'gx_0','gx_1','gz_1'}, dimensions={0} | all-to-all | bytes 32768 | tf_op jit(solution)/shard_map/all_to_all | solution.py:352
  107.2 18.8 %all_to_all.29.received = f32[32,1,128]{2,1,0:T(1,128)S(1)} all-to-all(f32[32,1,128]{2,1,0:T(1,128)S(1)} %broadcast_in_dim.17), channel_id=1, replica_groups=mesh['gx_0'=2,'gx_1'=2,'gy'=4,'gz_0'=8,'gz_1'=8] {'gy','gz_0'}, dimensions={0} | all-to-all | bytes 32768 | tf_op jit(solution)/shard_map/all_to_all | solution.py:352
  126.0 0.7 shard_map.83
  (9 shorter events, 0.1 us)
Async XLA Ops:
  27.2 19.6 %collective-permute-start = (f32[48,128]{1,0:T(8,128)S(1)}, f32[48,128]{1,0:T(8,128)S(1)}, u32[]{:S(2)}, u32[]{:S(2)}) collective-permute-start(f32[48,128]{1,0:T(8,128)S(1)} %get-tuple-element.18), channel_id=1, source_target_pairs={{0,1},{1,2},{2,3},{3,4},{4,5},{5,6},{6,7},{7,8},{8,9},{9,10},{10,1... | collective-permute-start | bytes 73736 | tf_op jit(solution)/shard_map/ppermute | solution.py:342
  29.2 17.7 %collective-permute-start.1 = (f32[48,128]{1,0:T(8,128)S(1)}, f32[48,128]{1,0:T(8,128)S(1)}, u32[]{:S(2)}, u32[]{:S(2)}) collective-permute-start(f32[48,128]{1,0:T(8,128)S(1)} %get-tuple-element.19), channel_id=1, source_target_pairs={{1,0},{2,1},{3,2},{4,3},{5,4},{6,5},{7,6},{8,7},{9,8},{10,9},{11,1... | collective-permute-start | bytes 73736 | tf_op jit(solution)/shard_map/ppermute | solution.py:347
  49.4 8.6 %collective-permute-start.2 = (f32[4,128]{1,0:T(4,128)S(1)}, f32[4,128]{1,0:T(4,128)S(1)}, u32[]{:S(2)}, u32[]{:S(2)}) collective-permute-start(f32[4,128]{1,0:T(4,128)S(1)} %get-tuple-element.24), channel_id=1, source_target_pairs={{0,1},{1,2},{2,3},{3,4},{4,5},{5,6},{6,7},{7,8},{8,9},{9,10},{10,1... | collective-permute-start | bytes 6152 | tf_op jit(solution)/shard_map/ppermute | solution.py:342
  51.4 7.4 %collective-permute-start.3 = (f32[4,128]{1,0:T(4,128)S(1)}, f32[4,128]{1,0:T(4,128)S(1)}, u32[]{:S(2)}, u32[]{:S(2)}) collective-permute-start(f32[4,128]{1,0:T(4,128)S(1)} %get-tuple-element.26), channel_id=1, source_target_pairs={{1,0},{2,1},{3,2},{4,3},{5,4},{6,5},{7,6},{8,7},{9,8},{10,9},{11,1... | collective-permute-start | bytes 6152 | tf_op jit(solution)/shard_map/ppermute | solution.py:347
  73.3 9.2 %collective-permute-start.4 = (f32[4,128]{1,0:T(4,128)S(1)}, f32[4,128]{1,0:T(4,128)S(1)}, u32[]{:S(2)}, u32[]{:S(2)}) collective-permute-start(f32[4,128]{1,0:T(4,128)S(1)} %get-tuple-element.29), channel_id=1, source_target_pairs={{0,1},{1,2},{2,3},{3,4},{4,5},{5,6},{6,7},{7,8},{8,9},{9,10},{10,1... | collective-permute-start | bytes 6152 | tf_op jit(solution)/shard_map/ppermute | solution.py:342
  75.2 7.9 %collective-permute-start.5 = (f32[4,128]{1,0:T(4,128)S(1)}, f32[4,128]{1,0:T(4,128)S(1)}, u32[]{:S(2)}, u32[]{:S(2)}) collective-permute-start(f32[4,128]{1,0:T(4,128)S(1)} %get-tuple-element.31), channel_id=1, source_target_pairs={{1,0},{2,1},{3,2},{4,3},{5,4},{6,5},{7,6},{8,7},{9,8},{10,9},{11,1... | collective-permute-start | bytes 6152 | tf_op jit(solution)/shard_map/ppermute | solution.py:347

commit v5 on v4

--- a/solution.py
+++ b/solution.py
@@ -17,7 +17,7 @@
 CELL_EDGE = 11.0
 CUTOFF = 10.0
 SCALE = 14.4 * 0.02 / CUTOFF**4
-FAR = 1.0e4
+FAR = 2.0**20
 ATOMS = 128
 GROUPS = ATOMS // 8
 FIELDS = 4
@@ -27,6 +27,11 @@
 VMEM = pltpu.VMEM
 HBM = pltpu.HBM
 F32 = jnp.float32
+BF16 = jnp.bfloat16
+DEPTH = 64
+PARTS = ((0, 0), (0, 1), (1, 0), (1, 1), (0, 2), (2, 0), (1, 2), (2, 1))
+CENTER = (CELL_EDGE / 2, CELL_EDGE, CELL_EDGE)
+CELLS = 24
 
 
 def run(body, outs, args, spaces=None, scratch=(), far=()):
@@ -85,30 +90,67 @@
     return jnp.where(kinds == 0.0, table[first : first + 1, :], table[first + 1 : first + 2, :])
 
 
-def place(near, index, lines, table, lift):
-    x, y, z, kinds = (jnp.broadcast_to(v, (8, ATOMS)) for v in lines)
-    near[0, index] = x
-    near[1, index] = y
-    near[2, index] = z + lift
-    near[3, index] = choose(kinds, table, 0)
-    near[4, index] = choose(kinds, table, 2)
+def parts_of(value):
+    one = value.astype(BF16).astype(F32)
+    rest = value - one
+    two = rest.astype(BF16).astype(F32)
+    return one, two, (rest - two).astype(BF16).astype(F32)
+
+
+def fill(coords, near, stack, dense, table, away):
+    for n in range(CELLS):
+        kinds = jnp.broadcast_to(coords[3, n : n + 1, :], (8, ATOMS))
+        near[0, n] = choose(kinds, table, 0)
+        near[1, n] = choose(kinds, table, 2)
+    stack[...] = jnp.zeros((CELLS * DEPTH, ATOMS), F32)
+
+    def put(row, value):
+        stack[pl.ds(row, CELLS, stride=DEPTH), :] = value
+
+    squares = jnp.zeros((CELLS, ATOMS), F32)
+    for axis in range(3):
+        value = coords[axis]
+        squares = squares + value * value
+        parts = parts_of(value)
+        for m, (_, theirs) in enumerate(PARTS):
+            put(8 * axis + m, parts[theirs])
+    for m, part in enumerate(parts_of(squares)):
+        put(24 + m, jnp.ones((CELLS, ATOMS), F32))
+        put(27 + m, part)
+    for tile in range(4):
+        put(30 + tile, away[tile])
+    for n in range(CELLS):
+        dense[n] = stack[n * DEPTH : (n + 1) * DEPTH, :].astype(BF16)
+
+
+def turn(tile, rows, turned):
+    turned[...] = jnp.zeros((ATOMS, ATOMS), F32)
+    squares = jnp.zeros((1, ATOMS), F32)
+    for axis in range(3):
+        value = rows[axis] - CENTER[axis]
+        squares = squares + value * value
+        parts = parts_of(value)
+        for m, (ours, _) in enumerate(PARTS):
+            turned[8 * axis + m : 8 * axis + m + 1, :] = -2.0 * parts[ours]
+    for m, part in enumerate(parts_of(squares)):
+        turned[24 + m : 25 + m, :] = part
+        turned[27 + m : 28 + m, :] = jnp.ones((1, ATOMS), F32)
+    turned[30 + tile : 31 + tile, :] = jnp.ones((1, ATOMS), F32)
+    return turned[...].T
 
 
 def row_sums(acc):
     return jnp.sum(acc.T, axis=0, keepdims=True)
 
 
-def couple(near, columns, away, tile, p, line, blocks, slot, sums_s, sums_t, mask):
-    xj = near[0, p] + away[tile, line : line + 1, :]
-    yj, zj, sj, cj = near[1, p], near[2, p], near[3, p], near[4, p]
+def couple(near, dense, terms, columns, tile, p, blocks, slot, sums_s, sums_t, mask):
+    sj, cj = near[0, p], near[1, p]
+    squares = jnp.dot(terms, dense[p], preferred_element_type=F32)
     for g in range(GROUPS):
         rows = pl.ds(g * 8, 8)
-        dx = xj - columns[tile, 0, rows, :]
-        dy = yj - columns[tile, 1, rows, :]
-        dz = zj - columns[tile, 2, rows, :]
-        r2 = dx * dx + dy * dy + dz * dz
+        r2 = squares[g * 8 : g * 8 + 8]
         r = r2 * lax.rsqrt(r2)
-        x = r2 * r + columns[tile, 3, rows, :] * sj
+        x = r2 * r + columns[tile, 1, rows, :] * sj
         inverse = jnp.exp2(lax.log2(x) * (-1.0 / 3.0))
         w = jnp.maximum(CUTOFF - r, 0.0)
         w2 = w * w
@@ -132,50 +174,44 @@
     return jnp.broadcast_to(jnp.where(found > 0.0, 0.0, FAR), (index.shape[0], ATOMS))
 
 
-def split(number, by, parts):
-    high = sum(jnp.where(number >= by * k, 1, 0) for k in range(1, parts))
-    return high, number - by * high
-
-
 def inner_body(
     received, own, neighbours, chi, eta, gamma,
-    blocks, acc, columns, away_outer, table, near, away,
+    blocks, acc, columns, away_outer, table, near, away, coords, stack, turned, dense,
 ):
     for kind in range(2):
         value = jnp.full((1, ATOMS), gamma[kind], F32)
         table[kind : kind + 1, :] = 1.0 / (value * jnp.sqrt(value))
         table[2 + kind : 3 + kind, :] = jnp.full((1, ATOMS), chi[kind], F32)
         table[4 + kind : 5 + kind, :] = jnp.full((1, ATOMS), eta[kind], F32)
+    cell = lax.broadcasted_iota(jnp.int32, (CELLS, 27), 0)
+    side = cell & 1
     for b in range(2):
         for c in range(2):
             tile = b * 2 + c
-            for field in range(FIELDS):
-                row = (c * 2 + b) * FIELDS + field
-                values = own[row : row + 1, :]
-                if field == 3:
-                    values = choose(values, table, 0)
-                columns[tile, field] = jnp.broadcast_to(values, (ATOMS, ATOMS)).T
+            row = (c * 2 + b) * FIELDS
+            columns[tile, 0] = turn(tile, [own[row + f : row + f + 1, :] for f in range(3)], turned)
+            shield = choose(own[row + 3 : row + 4, :], table, 0)
+            columns[tile, 1] = jnp.broadcast_to(shield, (ATOMS, ATOMS)).T
             entries = neighbours[0, b, c : c + 1, :]
-            slot = lax.broadcasted_iota(jnp.int32, (18, 27), 0)
-            ix, rest = split(slot, 6, 3)
-            jy, k = split(rest, 2, 3)
-            away[tile] = listed(entries, ix * 16 + (jy + b) * 4 + k + 1)
-            slot = lax.broadcasted_iota(jnp.int32, (9, 27), 0)
-            ix, jy = split(slot, 3, 3)
-            away_outer[tile] = listed(entries, ix * 16 + (jy + b) * 4 + 3 * c)
+            away[tile] = listed(entries, (cell - side) * 2 + side + 1)
+            away_outer[tile] = listed(entries, (cell - side) * 2 + side * 3)
     for ix, iy, peer, b, step in plane_columns():
         for k in range(2):
             row = (k * 2 + b) * FIELDS
-            lines = [received[peer, row + f : row + f + 1, :] for f in range(FIELDS)]
-            lines[0] = lines[0] + CELL_EDGE * (ix - 1)
-            lines[1] = lines[1] + CELL_EDGE * 2 * step
-            place(near, (ix * 4 + iy) * 2 + k, lines, table, 0.0)
+            n = (ix * 4 + iy) * 2 + k
+            shift = (CELL_EDGE * (ix - 1), CELL_EDGE * 2 * step, 0.0)
+            for axis in range(3):
+                line = received[peer, row + axis : row + axis + 1, :]
+                coords[axis, n : n + 1, :] = line + (shift[axis] - CENTER[axis])
+            coords[3, n : n + 1, :] = received[peer, row + 3 : row + 4, :]
+    fill(coords, near, stack, dense, table, away)
 
     lane = lax.broadcasted_iota(jnp.int32, (8, ATOMS), 1)
     sub = lax.broadcasted_iota(jnp.int32, (8, ATOMS), 0)
 
     def one_tile(tile, carry):
         b, c = tile // 2, tile % 2
+        terms = columns[tile, 0, :, 0:DEPTH].astype(BF16)
         sums_s = [jnp.zeros((8, ATOMS), F32) for _ in range(GROUPS)]
         sums_t = [jnp.zeros((8, ATOMS), F32) for _ in range(GROUPS)]
         for slot, (ix, jy, k) in enumerate(INNER):
@@ -184,7 +220,7 @@
                 first = jnp.where(c == k, 0, 2 * ATOMS)
                 mask = functools.partial(lambda at, g: lane == sub + (at + g * 8), first)
             p = (ix * 4 + jy + b) * 2 + k
-            couple(near, columns, away, tile, p, slot, blocks, slot, sums_s, sums_t, mask)
+            couple(near, dense, terms, columns, tile, p, blocks, slot, sums_s, sums_t, mask)
         store(acc, tile, sums_s, sums_t)
         return carry
 
@@ -193,23 +229,28 @@
 
 def outer_body(
     below, above, own, columns, away, table, partial,
-    blocks, out, head, tail, near, acc,
+    blocks, out, head, tail, near, acc, coords, stack, dense,
 ):
     for ix in range(3):
         for iy in range(4):
             line = (ix * 4 + iy) * FIELDS
             for side, (ghost, lift) in enumerate(((below, -2 * CELL_EDGE), (above, 2 * CELL_EDGE))):
-                lines = [ghost[line + f : line + f + 1, :] for f in range(FIELDS)]
-                place(near, (ix * 4 + iy) * 2 + side, lines, table, lift)
+                n = (ix * 4 + iy) * 2 + side
+                for axis in range(3):
+                    shift = (lift if axis == 2 else 0.0) - CENTER[axis]
+                    coords[axis, n : n + 1, :] = ghost[line + axis : line + axis + 1, :] + shift
+                coords[3, n : n + 1, :] = ghost[line + 3 : line + 4, :]
+    fill(coords, near, stack, dense, table, away)
 
     def one_tile(tile, carry):
         b, c = tile // 2, tile % 2
+        terms = columns[tile, 0, :, 0:DEPTH].astype(BF16)
         rows = [pl.ds(g * 8, 8) for g in range(GROUPS)]
         sums_s = [partial[tile, 0, r, :] for r in rows]
         sums_t = [partial[tile, 1, r, :] for r in rows]
         for slot, (ix, jy) in enumerate(OUTER):
             p = (ix * 4 + jy + b) * 2 + c
-            couple(near, columns, away, tile, p, slot, blocks, slot, sums_s, sums_t, None)
+            couple(near, dense, terms, columns, tile, p, blocks, slot, sums_s, sums_t, None)
         store(acc, tile, sums_s, sums_t)
         return carry
 
@@ -377,12 +418,16 @@
     below, above = upward(tail), downward(head)
     products = (4, 2, ATOMS, ATOMS)
     accumulate = VMEM(products, F32)
+    pairs = VMEM((2, CELLS, 8, ATOMS), F32)
+    cells = VMEM((4, CELLS, ATOMS), F32)
+    stack = VMEM((CELLS * DEPTH, ATOMS), F32)
+    dense = VMEM((CELLS, DEPTH, ATOMS), BF16)
     inner, partial, columns, away, table = run(
         inner_body,
-        [(4, 18, ATOMS, ATOMS), products, (4, FIELDS, ATOMS, ATOMS), (4, 9, ATOMS), (8, ATOMS)],
+        [(4, 18, ATOMS, ATOMS), products, (4, 2, ATOMS, ATOMS), (4, CELLS, ATOMS), (8, ATOMS)],
         (received, own, neighbours, type_chi, type_eta, type_gamma),
         [VMEM, VMEM, VMEM, smem, smem, smem],
-        [VMEM((5, 24, 8, ATOMS), F32), VMEM((4, 18, ATOMS), F32)],
+        [pairs, VMEM((4, CELLS, ATOMS), F32), cells, stack, VMEM((ATOMS, ATOMS), F32), dense],
         far=(2,),
     )
     vectors = [(8, ATOMS), (4, ATOMS), (4, ATOMS)]
@@ -390,7 +435,7 @@
         outer_body,
         [(4, 9, ATOMS, ATOMS)] + vectors,
         (below, above, own, columns, away, table, partial),
-        scratch=[VMEM((5, 24, 8, ATOMS), F32), accumulate],
+        scratch=[pairs, accumulate, cells, stack, dense],
     )
     near = VMEM((2, 48, 8, ATOMS), F32)
     received = surrounded(w1, head, tail)

time: 127 us -> 127 us (level)
  transfers between devices with their start and end apart: 6 -> 6, of which waited for: 2 -> 2; matrix products, arithmetic and copies ran while one was open for 0% -> 0% of each run, Pallas kernels for 5% -> 4%
where the time goes in v5:
time: 127 us
  blocking collectives  80 us (63%)
  starting transfers between devices  31.3 us (25%)
  Pallas kernels  13.1 us (10%)
  waiting for transfers between devices  1.42 us (1%)
    all_to_all x5, blocking collectives, shared(): lax.all_to_all(jnp.broadcast_to(block[None], (count,) + block.shape), axe...  80 us
    ppermute x3, starting transfers between devices, downward(): return lax.ppermute(head, GZ, [((i + 1) % count, i) for i in range(count)])  25.5 us
    pallas_call x6, Pallas kernels, run(): pl.pallas_call(body, out_shape=tuple((VMEM(shape, F32) for shape in outs)...  12.4 us
    ppermute x3, starting transfers between devices, upward(): return lax.ppermute(tail, GZ, [(i, (i + 1) % count) for i in range(count)])  5.76 us
  transfers between devices with their start and end apart: 6, of which 2 were waited for; matrix products, arithmetic and copies ran while one was open for 0% of the time, Pallas kernels for 4%

profile of v5, /device:TPU:1, one launch (start us, length us, event | category | flops | bytes accessed | tf_op | source)
XLA Modules:
  0.0 126.7 jit_solution(2620625656871028766)
XLA Ops:
  0.6 0.7 shard_map.77.own
  1.4 25.8 %all_to_all.25.received = f32[16,16,128]{2,1,0:T(8,128)S(1)} all-to-all(f32[16,16,128]{2,1,0:T(8,128)S(1)} %broadcast_in_dim.12), channel_id=1, replica_groups=mesh['gx_0'=2,'gx_1'=2,'gy'=4,'gz_0'=8,'gz_1'=8] {'gx_0','gx_1','gy'}, dimensions={0} | all-to-all | bytes 262144 | tf_op jit(solution)/shard_map/all_to_all | solution.py:393
  27.2 1.9 %collective-permute-start = (f32[48,128]{1,0:T(8,128)S(1)}, f32[48,128]{1,0:T(8,128)S(1)}, u32[]{:S(2)}, u32[]{:S(2)}) collective-permute-start(f32[48,128]{1,0:T(8,128)S(1)} %get-tuple-element.18), channel_id=1, source_target_pairs={{0,1},{1,2},{2,3},{3,4},{4,5},{5,6},{6,7},{7,8},{8,9},{9,10},{10,1... | collective-permute-start | bytes 73736 | tf_op jit(solution)/shard_map/ppermute | solution.py:383
  29.2 11.6 %collective-permute-start.1 = (f32[48,128]{1,0:T(8,128)S(1)}, f32[48,128]{1,0:T(8,128)S(1)}, u32[]{:S(2)}, u32[]{:S(2)}) collective-permute-start(f32[48,128]{1,0:T(8,128)S(1)} %get-tuple-element.19), channel_id=1, source_target_pairs={{1,0},{2,1},{3,2},{4,3},{5,4},{6,5},{7,6},{8,7},{9,8},{10,9},{11,1... | collective-permute-start | bytes 73736 | tf_op jit(solution)/shard_map/ppermute | solution.py:388
  40.8 5.6 %shard_map.79 = (f32[4,18,128,128]{3,2,1,0:T(8,128)S(1)}, f32[4,2,128,128]{3,2,1,0:T(8,128)S(1)}, f32[4,2,128,128]{3,2,1,0:T(8,128)S(1)}, f32[4,24,128]{2,1,0:T(8,128)S(1)}, f32[8,128]{1,0:T(8,128)S(1)}) custom-call(f32[16,16,128]{2,1,0:T(8,128)S(1)} %all_to_all.25.received, f32[16,128]{1,0:T(8,128)S(1)} %shard_map.77.own, s32[1,2,2,27]{3,2,1,0:T(2,128)} %neighbours.1, ...), custom_call_target="tpu_custom_call" | custom-call | tf_op jit(solution)/shard_map/pallas_call | solution.py:43
  46.4 0.0 collective-permute-done.below
  46.4 0.0 collective-permute-done.1.above
  46.4 2.9 %shard_map.80 = (f32[4,9,128,128]{3,2,1,0:T(8,128)S(1)}, f32[8,128]{1,0:T(8,128)S(1)}, f32[4,128]{1,0:T(4,128)S(1)}, f32[4,128]{1,0:T(4,128)S(1)}) custom-call(f32[48,128]{1,0:T(8,128)S(1)} %collective-permute-done.below, f32[48,128]{1,0:T(8,128)S(1)} %collective-permute-done.1.above, f32[16,128]{1,0:T(8,128)S(1)} %shard_map.77.own, ...), custom_call_target="tpu_custom_call" | custom-call | tf_op jit(solution)/shard_map/pallas_call | solution.py:43
  49.4 1.9 %collective-permute-start.2 = (f32[4,128]{1,0:T(4,128)S(1)}, f32[4,128]{1,0:T(4,128)S(1)}, u32[]{:S(2)}, u32[]{:S(2)}) collective-permute-start(f32[4,128]{1,0:T(4,128)S(1)} %get-tuple-element.24), channel_id=1, source_target_pairs={{0,1},{1,2},{2,3},{3,4},{4,5},{5,6},{6,7},{7,8},{8,9},{9,10},{10,1... | collective-permute-start | bytes 6152 | tf_op jit(solution)/shard_map/ppermute | solution.py:383
  51.3 6.7 %collective-permute-start.3 = (f32[4,128]{1,0:T(4,128)S(1)}, f32[4,128]{1,0:T(4,128)S(1)}, u32[]{:S(2)}, u32[]{:S(2)}) collective-permute-start(f32[4,128]{1,0:T(4,128)S(1)} %get-tuple-element.26), channel_id=1, source_target_pairs={{1,0},{2,1},{3,2},{4,3},{5,4},{6,5},{7,6},{8,7},{9,8},{10,9},{11,1... | collective-permute-start | bytes 6152 | tf_op jit(solution)/shard_map/ppermute | solution.py:388
  58.0 0.0 collective-permute-done.2
  58.0 0.7 collective-permute-done.3
  58.7 13.0 %all_to_all.26.received = f32[16,16,128]{2,1,0:T(8,128)S(1)} all-to-all(f32[16,16,128]{2,1,0:T(8,128)S(1)} %broadcast_in_dim.13), channel_id=1, replica_groups=mesh['gx_0'=2,'gx_1'=2,'gy'=4,'gz_0'=8,'gz_1'=8] {'gx_0','gx_1','gy'}, dimensions={0} | all-to-all | bytes 262144 | tf_op jit(solution)/shard_map/all_to_all | solution.py:393
  71.7 1.5 %shard_map.81 = (f32[8,128]{1,0:T(8,128)S(1)}, f32[4,128]{1,0:T(4,128)S(1)}, f32[4,128]{1,0:T(4,128)S(1)}) custom-call(f32[16,16,128]{2,1,0:T(8,128)S(1)} %all_to_all.26.received, f32[4,18,128,128]{3,2,1,0:T(8,128)S(1)} %get-tuple-element.27.inner, f32[4,9,128,128]{3,2,1,0:T(8,128)S(1)} %get-tuple-element.28.outer, f32[16,128]{1,0:T(8,128)S(1)} %shard_map.77.own, ...), custom_call_target="tpu_custom_call" | custom-call | tf_op jit(solution)/shard_map/pallas_call | solution.py:43
  73.2 1.9 %collective-permute-start.4 = (f32[4,128]{1,0:T(4,128)S(1)}, f32[4,128]{1,0:T(4,128)S(1)}, u32[]{:S(2)}, u32[]{:S(2)}) collective-permute-start(f32[4,128]{1,0:T(4,128)S(1)} %get-tuple-element.29), channel_id=1, source_target_pairs={{0,1},{1,2},{2,3},{3,4},{4,5},{5,6},{6,7},{7,8},{8,9},{9,10},{10,1... | collective-permute-start | bytes 6152 | tf_op jit(solution)/shard_map/ppermute | solution.py:383
  75.1 7.2 %collective-permute-start.5 = (f32[4,128]{1,0:T(4,128)S(1)}, f32[4,128]{1,0:T(4,128)S(1)}, u32[]{:S(2)}, u32[]{:S(2)}) collective-permute-start(f32[4,128]{1,0:T(4,128)S(1)} %get-tuple-element.31), channel_id=1, source_target_pairs={{1,0},{2,1},{3,2},{4,3},{5,4},{6,5},{7,6},{8,7},{9,8},{10,9},{11,1... | collective-permute-start | bytes 6152 | tf_op jit(solution)/shard_map/ppermute | solution.py:388
  82.4 0.0 collective-permute-done.4
  82.4 0.7 collective-permute-done.5
  83.1 12.4 %all_to_all.27.received = f32[16,16,128]{2,1,0:T(8,128)S(1)} all-to-all(f32[16,16,128]{2,1,0:T(8,128)S(1)} %broadcast_in_dim.14), channel_id=1, replica_groups=mesh['gx_0'=2,'gx_1'=2,'gy'=4,'gz_0'=8,'gz_1'=8] {'gx_0','gx_1','gy'}, dimensions={0} | all-to-all | bytes 262144 | tf_op jit(solution)/shard_map/all_to_all | solution.py:393
  95.5 1.6 %shard_map.82 = (f32[8,128]{1,0:T(8,128)S(1)}, f32[1,128]{1,0:T(1,128)S(1)}) custom-call(f32[16,16,128]{2,1,0:T(8,128)S(1)} %all_to_all.27.received, f32[4,18,128,128]{3,2,1,0:T(8,128)S(1)} %get-tuple-element.27.inner, f32[4,9,128,128]{3,2,1,0:T(8,128)S(1)} %get-tuple-element.28.outer, f32[16,128]{1,0:T(8,128)S(1)} %shard_map.77.own, ...), custom_call_target="tpu_custom_call" | custom-call | tf_op jit(solution)/shard_map/pallas_call | solution.py:43
  97.1 10.0 %all_to_all.28 = f32[32,1,128]{2,1,0:T(1,128)S(1)} all-to-all(f32[32,1,128]{2,1,0:T(1,128)S(1)} %broadcast_in_dim.16), channel_id=1, replica_groups=mesh['gx_0'=2,'gx_1'=2,'gy'=4,'gz_0'=8,'gz_1'=8] {'gx_0','gx_1','gz_1'}, dimensions={0} | all-to-all | bytes 32768 | tf_op jit(solution)/shard_map/all_to_all | solution.py:393
  107.2 18.8 %all_to_all.29.received = f32[32,1,128]{2,1,0:T(1,128)S(1)} all-to-all(f32[32,1,128]{2,1,0:T(1,128)S(1)} %broadcast_in_dim.17), channel_id=1, replica_groups=mesh['gx_0'=2,'gx_1'=2,'gy'=4,'gz_0'=8,'gz_1'=8] {'gy','gz_0'}, dimensions={0} | all-to-all | bytes 32768 | tf_op jit(solution)/shard_map/all_to_all | solution.py:393
  126.0 0.7 shard_map.83
  (9 shorter events, 0.1 us)
Async XLA Ops:
  27.2 19.2 %collective-permute-start = (f32[48,128]{1,0:T(8,128)S(1)}, f32[48,128]{1,0:T(8,128)S(1)}, u32[]{:S(2)}, u32[]{:S(2)}) collective-permute-start(f32[48,128]{1,0:T(8,128)S(1)} %get-tuple-element.18), channel_id=1, source_target_pairs={{0,1},{1,2},{2,3},{3,4},{4,5},{5,6},{6,7},{7,8},{8,9},{9,10},{10,1... | collective-permute-start | bytes 73736 | tf_op jit(solution)/shard_map/ppermute | solution.py:383
  29.2 17.3 %collective-permute-start.1 = (f32[48,128]{1,0:T(8,128)S(1)}, f32[48,128]{1,0:T(8,128)S(1)}, u32[]{:S(2)}, u32[]{:S(2)}) collective-permute-start(f32[48,128]{1,0:T(8,128)S(1)} %get-tuple-element.19), channel_id=1, source_target_pairs={{1,0},{2,1},{3,2},{4,3},{5,4},{6,5},{7,6},{8,7},{9,8},{10,9},{11,1... | collective-permute-start | bytes 73736 | tf_op jit(solution)/shard_map/ppermute | solution.py:388
  49.4 8.6 %collective-permute-start.2 = (f32[4,128]{1,0:T(4,128)S(1)}, f32[4,128]{1,0:T(4,128)S(1)}, u32[]{:S(2)}, u32[]{:S(2)}) collective-permute-start(f32[4,128]{1,0:T(4,128)S(1)} %get-tuple-element.24), channel_id=1, source_target_pairs={{0,1},{1,2},{2,3},{3,4},{4,5},{5,6},{6,7},{7,8},{8,9},{9,10},{10,1... | collective-permute-start | bytes 6152 | tf_op jit(solution)/shard_map/ppermute | solution.py:383
  51.3 7.4 %collective-permute-start.3 = (f32[4,128]{1,0:T(4,128)S(1)}, f32[4,128]{1,0:T(4,128)S(1)}, u32[]{:S(2)}, u32[]{:S(2)}) collective-permute-start(f32[4,128]{1,0:T(4,128)S(1)} %get-tuple-element.26), channel_id=1, source_target_pairs={{1,0},{2,1},{3,2},{4,3},{5,4},{6,5},{7,6},{8,7},{9,8},{10,9},{11,1... | collective-permute-start | bytes 6152 | tf_op jit(solution)/shard_map/ppermute | solution.py:388
  73.2 9.2 %collective-permute-start.4 = (f32[4,128]{1,0:T(4,128)S(1)}, f32[4,128]{1,0:T(4,128)S(1)}, u32[]{:S(2)}, u32[]{:S(2)}) collective-permute-start(f32[4,128]{1,0:T(4,128)S(1)} %get-tuple-element.29), channel_id=1, source_target_pairs={{0,1},{1,2},{2,3},{3,4},{4,5},{5,6},{6,7},{7,8},{8,9},{9,10},{10,1... | collective-permute-start | bytes 6152 | tf_op jit(solution)/shard_map/ppermute | solution.py:383
  75.1 7.9 %collective-permute-start.5 = (f32[4,128]{1,0:T(4,128)S(1)}, f32[4,128]{1,0:T(4,128)S(1)}, u32[]{:S(2)}, u32[]{:S(2)}) collective-permute-start(f32[4,128]{1,0:T(4,128)S(1)} %get-tuple-element.31), channel_id=1, source_target_pairs={{1,0},{2,1},{3,2},{4,3},{5,4},{6,5},{7,6},{8,7},{9,8},{10,9},{11,1... | collective-permute-start | bytes 6152 | tf_op jit(solution)/shard_map/ppermute | solution.py:388

commit v6 on v4

--- a/solution.py
+++ b/solution.py
@@ -11,8 +11,8 @@
 GX = ("gx_0", "gx_1")
 GZ = ("gz_0", "gz_1")
 PLANE = ("gx_0", "gx_1", "gy")
-GROUP_ONE = ("gx_0", "gx_1", "gz_1")
-GROUP_TWO = ("gy", "gz_0")
+GROUP_ONE = ("gy", "gz_0")
+GROUP_TWO = ("gx_0", "gx_1", "gz_1")
 
 CELL_EDGE = 11.0
 CUTOFF = 10.0

time: 127 us -> 129 us (1.016)
  blocking collectives: 80 us -> 81.4 us
    all_to_all x5, blocking collectives: 80 us -> 81.4 us  [shared(): lax.all_to_all(jnp.broadcast_to(block[None], (count,) + block.shape), axe...]
where the time goes in v6:
time: 129 us; the launch traced here: 128 us
  blocking collectives  81.4 us (63%)
  starting transfers between devices  31.3 us (24%)
  Pallas kernels  13.2 us (10%)
  waiting for transfers between devices  1.42 us (1%)
    all_to_all x5, blocking collectives, shared(): lax.all_to_all(jnp.broadcast_to(block[None], (count,) + block.shape), axe...  81.4 us
    ppermute x3, starting transfers between devices, downward(): return lax.ppermute(head, GZ, [((i + 1) % count, i) for i in range(count)])  25.5 us
    pallas_call x6, Pallas kernels, run(): pl.pallas_call(body, out_shape=tuple((VMEM(shape, F32) for shape in outs)...  12.4 us
    ppermute x3, starting transfers between devices, upward(): return lax.ppermute(tail, GZ, [(i, (i + 1) % count) for i in range(count)])  5.76 us
  transfers between devices with their start and end apart: 6, of which 2 were waited for; matrix products, arithmetic and copies ran while one was open for 0% of the time, Pallas kernels for 5%

profile of v6, /device:TPU:1, one launch (start us, length us, event | category | flops | bytes accessed | tf_op | source)
XLA Modules:
  0.0 128.2 jit_solution(4112404944898129939)
XLA Ops:
  0.6 0.7 shard_map.77.own
  1.4 25.8 %all_to_all.25.received = f32[16,16,128]{2,1,0:T(8,128)S(1)} all-to-all(f32[16,16,128]{2,1,0:T(8,128)S(1)} %broadcast_in_dim.12), channel_id=1, replica_groups=mesh['gx_0'=2,'gx_1'=2,'gy'=4,'gz_0'=8,'gz_1'=8] {'gx_0','gx_1','gy'}, dimensions={0} | all-to-all | bytes 262144 | tf_op jit(solution)/shard_map/all_to_all | solution.py:352
  27.2 1.9 %collective-permute-start = (f32[48,128]{1,0:T(8,128)S(1)}, f32[48,128]{1,0:T(8,128)S(1)}, u32[]{:S(2)}, u32[]{:S(2)}) collective-permute-start(f32[48,128]{1,0:T(8,128)S(1)} %get-tuple-element.18), channel_id=1, source_target_pairs={{0,1},{1,2},{2,3},{3,4},{4,5},{5,6},{6,7},{7,8},{8,9},{9,10},{10,1... | collective-permute-start | bytes 73736 | tf_op jit(solution)/shard_map/ppermute | solution.py:342
  29.2 11.6 %collective-permute-start.1 = (f32[48,128]{1,0:T(8,128)S(1)}, f32[48,128]{1,0:T(8,128)S(1)}, u32[]{:S(2)}, u32[]{:S(2)}) collective-permute-start(f32[48,128]{1,0:T(8,128)S(1)} %get-tuple-element.19), channel_id=1, source_target_pairs={{1,0},{2,1},{3,2},{4,3},{5,4},{6,5},{7,6},{8,7},{9,8},{10,9},{11,1... | collective-permute-start | bytes 73736 | tf_op jit(solution)/shard_map/ppermute | solution.py:347
  40.8 6.0 %shard_map.79 = (f32[4,18,128,128]{3,2,1,0:T(8,128)S(1)}, f32[4,2,128,128]{3,2,1,0:T(8,128)S(1)}, f32[4,4,128,128]{3,2,1,0:T(8,128)S(1)}, f32[4,9,128]{2,1,0:T(8,128)S(1)}, f32[8,128]{1,0:T(8,128)S(1)}) custom-call(f32[16,16,128]{2,1,0:T(8,128)S(1)} %all_to_all.25.received, f32[16,128]{1,0:T(8,128)S(1)} %shard_map.77.own, s32[1,2,2,27]{3,2,1,0:T(2,128)} %neighbours.1, ...), custom_call_target="tpu_custom_call" | custom-call | tf_op jit(solution)/shard_map/pallas_call | solution.py:38
  46.8 0.0 collective-permute-done.below
  46.8 0.0 collective-permute-done.1.above
  46.8 2.6 %shard_map.80 = (f32[4,9,128,128]{3,2,1,0:T(8,128)S(1)}, f32[8,128]{1,0:T(8,128)S(1)}, f32[4,128]{1,0:T(4,128)S(1)}, f32[4,128]{1,0:T(4,128)S(1)}) custom-call(f32[48,128]{1,0:T(8,128)S(1)} %collective-permute-done.below, f32[48,128]{1,0:T(8,128)S(1)} %collective-permute-done.1.above, f32[16,128]{1,0:T(8,128)S(1)} %shard_map.77.own, ...), custom_call_target="tpu_custom_call" | custom-call | tf_op jit(solution)/shard_map/pallas_call | solution.py:38
  49.4 1.9 %collective-permute-start.2 = (f32[4,128]{1,0:T(4,128)S(1)}, f32[4,128]{1,0:T(4,128)S(1)}, u32[]{:S(2)}, u32[]{:S(2)}) collective-permute-start(f32[4,128]{1,0:T(4,128)S(1)} %get-tuple-element.24), channel_id=1, source_target_pairs={{0,1},{1,2},{2,3},{3,4},{4,5},{5,6},{6,7},{7,8},{8,9},{9,10},{10,1... | collective-permute-start | bytes 6152 | tf_op jit(solution)/shard_map/ppermute | solution.py:342
  51.4 6.7 %collective-permute-start.3 = (f32[4,128]{1,0:T(4,128)S(1)}, f32[4,128]{1,0:T(4,128)S(1)}, u32[]{:S(2)}, u32[]{:S(2)}) collective-permute-start(f32[4,128]{1,0:T(4,128)S(1)} %get-tuple-element.26), channel_id=1, source_target_pairs={{1,0},{2,1},{3,2},{4,3},{5,4},{6,5},{7,6},{8,7},{9,8},{10,9},{11,1... | collective-permute-start | bytes 6152 | tf_op jit(solution)/shard_map/ppermute | solution.py:347
  58.1 0.0 collective-permute-done.2
  58.1 0.7 collective-permute-done.3
  58.8 13.0 %all_to_all.26.received = f32[16,16,128]{2,1,0:T(8,128)S(1)} all-to-all(f32[16,16,128]{2,1,0:T(8,128)S(1)} %broadcast_in_dim.13), channel_id=1, replica_groups=mesh['gx_0'=2,'gx_1'=2,'gy'=4,'gz_0'=8,'gz_1'=8] {'gx_0','gx_1','gy'}, dimensions={0} | all-to-all | bytes 262144 | tf_op jit(solution)/shard_map/all_to_all | solution.py:352
  71.8 1.5 %shard_map.81 = (f32[8,128]{1,0:T(8,128)S(1)}, f32[4,128]{1,0:T(4,128)S(1)}, f32[4,128]{1,0:T(4,128)S(1)}) custom-call(f32[16,16,128]{2,1,0:T(8,128)S(1)} %all_to_all.26.received, f32[4,18,128,128]{3,2,1,0:T(8,128)S(1)} %get-tuple-element.27.inner, f32[4,9,128,128]{3,2,1,0:T(8,128)S(1)} %get-tuple-element.28.outer, f32[16,128]{1,0:T(8,128)S(1)} %shard_map.77.own, ...), custom_call_target="tpu_custom_call" | custom-call | tf_op jit(solution)/shard_map/pallas_call | solution.py:38
  73.3 1.9 %collective-permute-start.4 = (f32[4,128]{1,0:T(4,128)S(1)}, f32[4,128]{1,0:T(4,128)S(1)}, u32[]{:S(2)}, u32[]{:S(2)}) collective-permute-start(f32[4,128]{1,0:T(4,128)S(1)} %get-tuple-element.29), channel_id=1, source_target_pairs={{0,1},{1,2},{2,3},{3,4},{4,5},{5,6},{6,7},{7,8},{8,9},{9,10},{10,1... | collective-permute-start | bytes 6152 | tf_op jit(solution)/shard_map/ppermute | solution.py:342
  75.2 7.2 %collective-permute-start.5 = (f32[4,128]{1,0:T(4,128)S(1)}, f32[4,128]{1,0:T(4,128)S(1)}, u32[]{:S(2)}, u32[]{:S(2)}) collective-permute-start(f32[4,128]{1,0:T(4,128)S(1)} %get-tuple-element.31), channel_id=1, source_target_pairs={{1,0},{2,1},{3,2},{4,3},{5,4},{6,5},{7,6},{8,7},{9,8},{10,9},{11,1... | collective-permute-start | bytes 6152 | tf_op jit(solution)/shard_map/ppermute | solution.py:347
  82.4 0.0 collective-permute-done.4
  82.4 0.7 collective-permute-done.5
  83.2 12.4 %all_to_all.27.received = f32[16,16,128]{2,1,0:T(8,128)S(1)} all-to-all(f32[16,16,128]{2,1,0:T(8,128)S(1)} %broadcast_in_dim.14), channel_id=1, replica_groups=mesh['gx_0'=2,'gx_1'=2,'gy'=4,'gz_0'=8,'gz_1'=8] {'gx_0','gx_1','gy'}, dimensions={0} | all-to-all | bytes 262144 | tf_op jit(solution)/shard_map/all_to_all | solution.py:352
  95.6 1.6 %shard_map.82 = (f32[8,128]{1,0:T(8,128)S(1)}, f32[1,128]{1,0:T(1,128)S(1)}) custom-call(f32[16,16,128]{2,1,0:T(8,128)S(1)} %all_to_all.27.received, f32[4,18,128,128]{3,2,1,0:T(8,128)S(1)} %get-tuple-element.27.inner, f32[4,9,128,128]{3,2,1,0:T(8,128)S(1)} %get-tuple-element.28.outer, f32[16,128]{1,0:T(8,128)S(1)} %shard_map.77.own, ...), custom_call_target="tpu_custom_call" | custom-call | tf_op jit(solution)/shard_map/pallas_call | solution.py:38
  97.2 14.0 %all_to_all.28 = f32[32,1,128]{2,1,0:T(1,128)S(1)} all-to-all(f32[32,1,128]{2,1,0:T(1,128)S(1)} %broadcast_in_dim.16), channel_id=1, replica_groups=mesh['gx_0'=2,'gx_1'=2,'gy'=4,'gz_0'=8,'gz_1'=8] {'gy','gz_0'}, dimensions={0} | all-to-all | bytes 32768 | tf_op jit(solution)/shard_map/all_to_all | solution.py:352
  111.2 16.2 %all_to_all.29.received = f32[32,1,128]{2,1,0:T(1,128)S(1)} all-to-all(f32[32,1,128]{2,1,0:T(1,128)S(1)} %broadcast_in_dim.17), channel_id=1, replica_groups=mesh['gx_0'=2,'gx_1'=2,'gy'=4,'gz_0'=8,'gz_1'=8] {'gx_0','gx_1','gz_1'}, dimensions={0} | all-to-all | bytes 32768 | tf_op jit(solution)/shard_map/all_to_all | solution.py:352
  127.4 0.7 shard_map.83
  (9 shorter events, 0.1 us)
Async XLA Ops:
  27.2 19.6 %collective-permute-start = (f32[48,128]{1,0:T(8,128)S(1)}, f32[48,128]{1,0:T(8,128)S(1)}, u32[]{:S(2)}, u32[]{:S(2)}) collective-permute-start(f32[48,128]{1,0:T(8,128)S(1)} %get-tuple-element.18), channel_id=1, source_target_pairs={{0,1},{1,2},{2,3},{3,4},{4,5},{5,6},{6,7},{7,8},{8,9},{9,10},{10,1... | collective-permute-start | bytes 73736 | tf_op jit(solution)/shard_map/ppermute | solution.py:342
  29.2 17.7 %collective-permute-start.1 = (f32[48,128]{1,0:T(8,128)S(1)}, f32[48,128]{1,0:T(8,128)S(1)}, u32[]{:S(2)}, u32[]{:S(2)}) collective-permute-start(f32[48,128]{1,0:T(8,128)S(1)} %get-tuple-element.19), channel_id=1, source_target_pairs={{1,0},{2,1},{3,2},{4,3},{5,4},{6,5},{7,6},{8,7},{9,8},{10,9},{11,1... | collective-permute-start | bytes 73736 | tf_op jit(solution)/shard_map/ppermute | solution.py:347
  49.4 8.6 %collective-permute-start.2 = (f32[4,128]{1,0:T(4,128)S(1)}, f32[4,128]{1,0:T(4,128)S(1)}, u32[]{:S(2)}, u32[]{:S(2)}) collective-permute-start(f32[4,128]{1,0:T(4,128)S(1)} %get-tuple-element.24), channel_id=1, source_target_pairs={{0,1},{1,2},{2,3},{3,4},{4,5},{5,6},{6,7},{7,8},{8,9},{9,10},{10,1... | collective-permute-start | bytes 6152 | tf_op jit(solution)/shard_map/ppermute | solution.py:342
  51.4 7.4 %collective-permute-start.3 = (f32[4,128]{1,0:T(4,128)S(1)}, f32[4,128]{1,0:T(4,128)S(1)}, u32[]{:S(2)}, u32[]{:S(2)}) collective-permute-start(f32[4,128]{1,0:T(4,128)S(1)} %get-tuple-element.26), channel_id=1, source_target_pairs={{1,0},{2,1},{3,2},{4,3},{5,4},{6,5},{7,6},{8,7},{9,8},{10,9},{11,1... | collective-permute-start | bytes 6152 | tf_op jit(solution)/shard_map/ppermute | solution.py:347
  73.3 9.2 %collective-permute-start.4 = (f32[4,128]{1,0:T(4,128)S(1)}, f32[4,128]{1,0:T(4,128)S(1)}, u32[]{:S(2)}, u32[]{:S(2)}) collective-permute-start(f32[4,128]{1,0:T(4,128)S(1)} %get-tuple-element.29), channel_id=1, source_target_pairs={{0,1},{1,2},{2,3},{3,4},{4,5},{5,6},{6,7},{7,8},{8,9},{9,10},{10,1... | collective-permute-start | bytes 6152 | tf_op jit(solution)/shard_map/ppermute | solution.py:342
  75.2 7.9 %collective-permute-start.5 = (f32[4,128]{1,0:T(4,128)S(1)}, f32[4,128]{1,0:T(4,128)S(1)}, u32[]{:S(2)}, u32[]{:S(2)}) collective-permute-start(f32[4,128]{1,0:T(4,128)S(1)} %get-tuple-element.31), channel_id=1, source_target_pairs={{1,0},{2,1},{3,2},{4,3},{5,4},{6,5},{7,6},{8,7},{9,8},{10,9},{11,1... | collective-permute-start | bytes 6152 | tf_op jit(solution)/shard_map/ppermute | solution.py:347
